TPU v7x, 512 devices: a whole 4x4x16 slice. The times are simulated.
512 devices in a mesh: gossip: 16 (over x_lo, y, core), fsdp: 32 (over z, x_hi).
Axes of the slice: x: 4 (x_hi: 2, x_lo: 2; x = x_hi * 2 + x_lo), y: 4, z: 16, core: 2. Of those that a mesh axis runs over, the one named last changes fastest.
Arguments:
- activations: bfloat16 [16, 4096, 4608], P('gossip', 'fsdp'), may hold values from -6 to 6
- norm_gain: float32 [16, 4608], P('gossip'), may hold values from -0.5 to 1
- key_grad: bfloat16 [16, 4096, 1024], P('gossip', 'fsdp'), may hold values from -6 to 6
- numerator: float32 [16, 4608, 1024], P('gossip', 'fsdp'), may hold values from -6 to 6
- push_weight: float32 [16], P('gossip'), may hold values from 0.5 to 2
- step_count: int32 [1], replicated, may hold values from 0 to 999
Outputs:
- keys: bfloat16 [16, 4096, 1024], P('gossip', 'fsdp')
- input_grad: bfloat16 [16, 4096, 4608], P('gossip', 'fsdp')
- new_numerator: float32 [16, 4608, 1024], P('gossip', 'fsdp')
- new_weight: float32 [16], P('gossip')
All inputs are finite; a program needn't handle non-finite values.
Results may differ from a plain program's by a relative error of at most 0.0085.
Values may be sent and summed in bfloat16 or wider, within the bound.
No kernel may reach another device: no remote copies, remote signals or barrier semaphores. Data moves between devices by JAX's collectives and lax.ppermute only.
A program may use at most 128 MiB of HBM per device.

v0:
```python
from functools import partial
import math

import jax
import jax.numpy as jnp
from jax import lax
from jax.sharding import PartitionSpec as P

learn_rate = 0.01


def shortened(x):
    return jax.tree.map(lambda a: a.astype(jnp.bfloat16) if a.dtype == jnp.float32 else a, x)


def shifted(block, axis, distance):
    devices = range(lax.axis_size(axis))
    route = [((i - distance) % len(devices), i) for i in devices]
    return lax.ppermute(block, axis, route)


def send_state(numer_rows, weight_now, distance):
    return (
        shifted(shortened(numer_rows), "gossip", distance).astype(numer_rows.dtype),
        shifted(shortened(weight_now), "gossip", distance).astype(weight_now.dtype),
    )


def gossip_message(numer_rows, weight_now, step_count):
    levels = lax.axis_size("gossip").bit_length() - 1
    chosen = lax.rem(step_count[0], levels)
    branches = [partial(send_state, distance=2**level) for level in range(levels)]
    return lax.switch(chosen, branches, numer_rows, weight_now)


def local(activations, norm_gain, key_grad, numerator, push_weight, step_count):
    rows_in = activations[0]
    gain_row = norm_gain[0]
    grad_keys = key_grad[0]
    numer_rows = numerator[0]
    width = rows_in.shape[1]
    param = (numer_rows / (push_weight[0] * math.sqrt(width))).astype(jnp.bfloat16)
    values = rows_in.astype(jnp.float32)
    inv_rms = lax.rsqrt(jnp.mean(values * values, axis=-1, keepdims=True) + 1e-06)
    unit = values * inv_rms
    factor = 1.0 + gain_row
    normed = (unit * factor).astype(jnp.bfloat16)
    full_weight = lax.all_gather(param, "fsdp", axis=0, tiled=True)
    keys = jnp.dot(normed, full_weight, preferred_element_type=jnp.float32).astype(jnp.bfloat16)
    all_grads = lax.all_gather(grad_keys, "fsdp", axis=0, tiled=True)
    normed_cols = lax.all_to_all(normed, "fsdp", split_axis=1, concat_axis=0, tiled=True)
    grad_rows = lax.dot_general(
        normed_cols, all_grads, (((0,), (0,)), ((), ())), preferred_element_type=jnp.float32
    )
    dnormed = lax.dot_general(
        grad_keys, full_weight, (((1,), (1,)), ((), ())), preferred_element_type=jnp.float32
    ).astype(jnp.bfloat16)
    scaled = dnormed.astype(jnp.float32) * factor
    input_grad = (
        inv_rms * (scaled - unit * jnp.mean(scaled * unit, axis=-1, keepdims=True))
    ).astype(jnp.bfloat16)
    peer_numer, peer_weight = gossip_message(numer_rows, push_weight, step_count)
    new_numerator = 0.5 * (numer_rows - learn_rate * grad_rows) + 0.5 * peer_numer
    new_weight = 0.5 * (push_weight + peer_weight)
    return (keys[None], input_grad[None], new_numerator[None], new_weight)


def solution(mesh):
    return jax.shard_map(
        local,
        mesh=mesh,
        in_specs=(
            P("gossip", "fsdp", None),
            P("gossip", None),
            P("gossip", "fsdp", None),
            P("gossip", "fsdp", None),
            P("gossip"),
            P(),
        ),
        out_specs=(
            P("gossip", "fsdp", None),
            P("gossip", "fsdp", None),
            P("gossip", "fsdp", None),
            P("gossip"),
        ),
        check_vma=False,
    )
```

profile of v0, /device:TPU:24, one launch (start us, length us, event | category | flops | bytes accessed | tf_op | source)
XLA Modules:
  0.0 460.4 jit_solution(10469854523785945964)
XLA Ops:
  7.2 0.0 copy-start.3
  7.2 0.0 all-gather.6.cloned.1.call-start
  7.2 0.7 all-gather.6.cloned.1.call-update
  7.9 0.0 all-gather.4.cloned.1.call-start
  8.6 1.9 divide_convert_fusion
  10.5 0.0 all-gather.4.cloned.1.call-update
  10.5 1.7 copy.16
  12.2 0.0 copy-done.3
  12.2 0.1 add_reduce_fusion
  12.3 0.0 copy-start.1
  12.3 0.1 mul.97
  12.4 0.6 fusion.5
  13.0 0.0 copy-done.1
  13.0 0.0 copy-start
  13.0 1.6 multiply_convert_fusion
  14.6 17.9 %all-to-all-start = ((bf16[128,32,144]{0,2,1:T(8,128)(2,1)}), bf16[128,32,144]{0,2,1:T(8,128)(2,1)S(1)}, u32[]{:S(2)}, u32[]{:S(2)}) async-start(bf16[128,32,144]{0,2,1:T(8,128)(2,1)} %multiply_convert_fusion), calls=%async_computation | async-start | bytes 2359296 | tf_op jit(solution)/shard_map/all_to_all | solution.py:51
  33.2 0.0 copy-done
  33.2 8.9 %conditional.4 = (f32[144,1024]{1,0:T(8,128)S(1)}, f32[1]{0:T(128)}) conditional(s32[]{:T(128)} %clamp.3, (f32[144,1024]{1,0:T(8,128)S(1)}, f32[1]{0:T(128)}) %tuple.77, (f32[144,1024]{1,0:T(8,128)S(1)}, f32[1]{0:T(128)}) %tuple.78, (f32[144,1024]{1,0:T(8,128)S(1)}, f32[1]{0:T(128)}) %tuple.79, ...), branch_computations={%region_2.0_spmd, %region_3.0_spmd, %region_4.0_spmd, %region_5.0_... | conditional | flops 294914 | bytes 2949236
  33.3 1.9 collective-permute-start
  35.8 3.1 collective-permute-start.1
  38.9 2.4 collective-permute-done.1
  42.0 0.0 collective-permute-done
  42.1 61.5 %all-to-all-done = bf16[128,32,144]{0,2,1:T(8,128)(2,1)S(1)} async-done(((bf16[128,32,144]{0,2,1:T(8,128)(2,1)}), bf16[128,32,144]{0,2,1:T(8,128)(2,1)S(1)}, u32[]{:S(2)}, u32[]{:S(2)}) %all-to-all-start) | async-done | bytes 1179680 | tf_op jit(solution)/shard_map/all_to_all | solution.py:51
  103.6 137.1 %all-gather.6.cloned.1.call-done = bf16[1,4096,1024]{2,1,0:T(8,128)(2,1)} async-done(((bf16[1,128,1024]{2,1,0:T(8,128)(2,1)}), bf16[1,4096,1024]{2,1,0:T(8,128)(2,1)}) %all-gather.6.cloned.1.call-update) | async-done | bytes 8388624 | tf_op jit(solution)/shard_map/all_gather | solution.py:50
  240.8 5.6 %fusion.18 = f32[1,144,1024]{2,1,0:T(8,128)} fusion(f32[144,1024]{1,0:T(8,128)S(1)} %get-tuple-element.60, bf16[1,4096,1024]{2,1,0:T(8,128)(2,1)} %all-gather.6.cloned.1.call-done, f32[1,144,1024]{2,1,0:T(8,128)S(1)} %copy-done, bf16[128,32,144]{0,2,1:T(8,128)(2,1)S(1)} %all-to-all-done), kind=kOutput, calls=%fused_computation.17 | convolution fusion | flops 1208549376 | bytes 11337728 | tf_op jit(solution)/shard_map/dot_general | solution.py:52
  246.4 192.4 %all-gather.4.cloned.1.call-done = bf16[4608,1024]{1,0:T(8,128)(2,1)} async-done(((bf16[144,1024]{1,0:T(8,128)(2,1)}), bf16[4608,1024]{1,0:T(8,128)(2,1)}) %all-gather.4.cloned.1.call-update) | async-done | bytes 9437200 | tf_op jit(solution)/shard_map/all_gather | solution.py:48
  438.8 5.4 %multiply_reduce_fusion = (f32[128]{0:T(128)S(1)}, f32[128,4608]{0,1:T(8,128)S(1)}) fusion(bf16[1,128,4608]{1,2,0:T(8,128)(2,1)S(1)} %copy.16, f32[128]{0:T(128)S(1)} %add_rsqrt_fusion, f32[4608]{0:T(1024)} %copy-done.1, bf16[4608,1024]{1,0:T(8,128)(2,1)} %all-gather.4.cloned.1.call-done, bf16[1,128,1024]{2,1,0:T(8,128)(2,1)} %param.12), kind=kOutput, calls=%fused_computation.11 | convolution fusion | flops 1212088192 | bytes 13257728 | tf_op jit(solution)/shard_map/dot_general | solution.py:55
  444.3 0.5 fusion.21
  444.7 0.0 copy-start.2
  444.7 1.4 copy.18
  446.1 0.0 copy-done.2
  446.2 6.2 %fusion.26 = bf16[1,128,1024]{2,1,0:T(8,128)(2,1)} fusion(bf16[4608,1024]{1,0:T(8,128)(2,1)} %all-gather.4.cloned.1.call-done, bf16[1,128,4608]{1,2,0:T(8,128)(2,1)S(1)} %copy.16, f32[4608]{0:T(1024)S(1)} %copy-done.2, f32[128]{0:T(128)S(1)} %add_rsqrt_fusion), kind=kOutput, calls=%fused_computation.24 | convolution fusion | flops 1210449920 | bytes 10897920 | tf_op jit(solution)/shard_map/dot_general | solution.py:49
  (4 shorter events, 0.1 us)
Async XLA Ops:
  7.2 5.0 %copy-start.3 = (f32[1,4608]{1,0:T(1,128)S(1)}, f32[1,4608]{1,0:T(1,128)}, u32[]{:S(2)}) copy-start(f32[1,4608]{1,0:T(1,128)} %param.11) | copy-start | bytes 55300
  7.2 233.6 %all-gather.6.cloned.1.call-start = ((), (), s32[]{:S(2)}) async-start(), calls=%async_computation.2 | async-start | bytes 8650752 | tf_op jit(solution)/shard_map/all_gather | solution.py:50
  7.9 430.9 %all-gather.4.cloned.1.call-start = ((), (), s32[]{:S(2)}) async-start(), calls=%async_computation.1 | async-start | bytes 9732096 | tf_op jit(solution)/shard_map/all_gather | solution.py:48
  12.3 0.7 copy-start.1
  13.0 20.2 %copy-start = (f32[1,144,1024]{2,1,0:T(8,128)S(1)}, f32[1,144,1024]{2,1,0:T(8,128)}, u32[]{:S(2)}) copy-start(f32[1,144,1024]{2,1,0:T(8,128)} %param.13) | copy-start | bytes 1769476
  14.6 89.1 %all-to-all-start = ((bf16[128,32,144]{0,2,1:T(8,128)(2,1)}), bf16[128,32,144]{0,2,1:T(8,128)(2,1)S(1)}, u32[]{:S(2)}, u32[]{:S(2)}) async-start(bf16[128,32,144]{0,2,1:T(8,128)(2,1)} %multiply_convert_fusion), calls=%async_computation | async-start | bytes 2359296 | tf_op jit(solution)/shard_map/all_to_all | solution.py:51
  33.3 8.8 %collective-permute-start = (bf16[144,1024]{1,0:T(8,128)(2,1)S(1)}, bf16[144,1024]{1,0:T(8,128)(2,1)S(1)}, u32[]{:S(2)}, u32[]{:S(2)}) collective-permute-start(bf16[144,1024]{1,0:T(8,128)(2,1)S(1)} %convert_element_type.76), channel_id=1, source_target_pairs={{480,0},{0,32},{32,64},{64,96},{96,128},{128,160},{160,192},{192,2... | collective-permute-start | bytes 884744 | tf_op jit(solution)/shard_map/cond/branch_0_fun/ppermute | solution.py:19
  35.8 5.5 %collective-permute-start.1 = (bf16[1]{0:T(256)(128)(2,1)}, bf16[1]{0:T(256)(128)(2,1)}, u32[]{:S(2)}, u32[]{:S(2)}) collective-permute-start(bf16[1]{0:T(256)(128)(2,1)} %convert_element_type.78), channel_id=1, source_target_pairs={{480,0},{0,32},{32,64},{64,96},{96,128},{128,160},{160,192},{192,2... | collective-permute-start | bytes 14 | tf_op jit(solution)/shard_map/cond/branch_0_fun/ppermute | solution.py:19
  444.7 1.4 copy-start.2
Sparse Core Ops, SparseCore 0:
  11.1 229.6 all-gather.5
  243.9 194.9 all-gather.3
where the time goes:
time: 461 us; the launch traced here: 460 us
  waiting for transfers between devices  394 us (85%)
  starting transfers between devices  23 us (5%)
  matrix products  17.3 us (4%)
  between operations  16.6 us (4%)
  other arithmetic  4.67 us (1%)
    all_gather x1, waiting for transfers between devices, local(): full_weight = lax.all_gather(param, 'fsdp', axis=0, tiled=True)  192 us
    all_gather x1, waiting for transfers between devices, local(): all_grads = lax.all_gather(grad_keys, 'fsdp', axis=0, tiled=True)  137 us
    all_to_all x1, waiting for transfers between devices, local(): lax.all_to_all(normed, 'fsdp', split_axis=1, concat_axis=0, tiled=True)  61.5 us
    all_to_all x1, starting transfers between devices, local(): lax.all_to_all(normed, 'fsdp', split_axis=1, concat_axis=0, tiled=True)  17.9 us
  transfers between devices with their start and end apart: 5, of which 4 were waited for; matrix products, arithmetic and copies ran while one was open for 3% of the time, Pallas kernels for 0%

commit v1 on v0

v1 whole, which is shorter than its diff:
```python
from functools import partial
import math

import jax
import jax.numpy as jnp
from jax import lax
from jax.experimental import pallas as pl
from jax.experimental.pallas import tpu as pltpu
from jax.sharding import Mesh, PartitionSpec as P

learn_rate = 0.01
bf16, f32 = jnp.bfloat16, jnp.float32
LANES = 128
TN = (((0,), (0,)), ((), ()))
NT = (((1,), (1,)), ((), ()))


def sent(block, axis, distance):
    count = lax.axis_size(axis)
    return lax.ppermute(block, axis, [(i, (i + distance) % count) for i in range(count)])


def together(*arrays):
    return lax.optimization_barrier(arrays)


def lanes(b):
    return pl.ds(b * LANES, LANES)


def call(body, outs, scratch=(), flops=0, size=0):
    shapes = [jax.ShapeDtypeStruct(s, d) for s, d in outs]

    def run(*arrays):
        spaces = [pltpu.SMEM if a.size < 3 else pltpu.VMEM for a in arrays]
        return pl.pallas_call(
            body,
            out_shape=shapes,
            in_specs=[pl.BlockSpec(memory_space=space) for space in spaces],
            out_specs=[pl.BlockSpec(memory_space=pltpu.VMEM)] * len(outs),
            scratch_shapes=list(scratch),
            compiler_params=pltpu.CompilerParams(vmem_limit_bytes=32 * 2**20),
            cost_estimate=pl.CostEstimate(flops=flops, bytes_accessed=size, transcendentals=0),
        )(*arrays)

    return run


def block(rows, place):
    return pl.ds(place * rows, rows)


def owned(rows, owner):
    return pl.ds(pl.multiple_of(owner * rows, 16), rows)


def block(rows, place):
    return pl.ds(place * rows, rows)


def owned(rows, owner):
    return pl.ds(pl.multiple_of(owner * rows, 16), rows)


def normalise(rows, ring, at, push, act, gain, grads, numer, mine, send, inv, param, message, turned):
    param[...] = (numer[...] / (push[0] * math.sqrt(act.shape[1]))).astype(bf16)
    message[pl.ds(0, rows), :] = numer[...].astype(bf16)
    message[pl.ds(rows, 16), :] = jnp.full((16, numer.shape[1]), push[0], f32).astype(bf16)
    (tokens, width), z, h = act.shape, at[0], at[1]
    squares = jnp.zeros((tokens, LANES), f32)
    for b in range(width // LANES):
        x = act[:, lanes(b)].astype(f32)
        squares = squares + x * x
    scale = lax.rsqrt(jnp.sum(squares, axis=1, keepdims=True) / width + 1e-06)
    inv[...] = scale
    for b in range(width // LANES):
        unit = act[:, lanes(b)].astype(f32) * scale
        turned[lanes(b), :] = (unit * (1.0 + gain[:, lanes(b)])).T.astype(bf16)
    for place in range(ring):
        owner = lax.rem(z + place, ring)
        mine[block(rows, place), :] = turned[owned(rows, 2 * owner + h), :]
        send[block(rows, place), :] = turned[owned(rows, 2 * owner + 1 - h), :]
    for b in range(grads.shape[1] // LANES):
        send[pl.ds(width // 2 + b * tokens, tokens), :] = grads[:, lanes(b)]


def outer(rows, ring, at, mine, peer, grads, up, down, both):
    tokens, features = grads.shape
    both[pl.ds(0, tokens), :] = grads[...]
    for b in range(features // LANES):
        both[pl.ds(tokens, tokens), lanes(b)] = peer[pl.ds(mine.shape[0] + b * tokens, tokens), :]
    for place in range(ring):
        of = block(rows, place)
        normed = jnp.concatenate([mine[of, :], peer[of, :]], axis=1)
        product = jnp.dot(normed, both[...], preferred_element_type=f32).astype(bf16)
        if place < ring // 2:
            up[of, :] = product
        else:
            down[block(rows, place - ring // 2), :] = product


def project(rows, ring, at, mine, peer, both, *refs):
    blocks, (own, send, keys, total) = refs[:ring], refs[ring:]
    tokens, (half, features) = mine.shape[1], (mine.shape[0], both.shape[1])
    for place in range(ring):
        of = block(rows, place)
        weight = blocks[place][...]
        dnormed = lax.dot_general(weight, both[...], NT, preferred_element_type=f32).astype(bf16)
        own[of, :] = dnormed[:, :tokens]
        send[of, :] = dnormed[:, tokens:]
        normed = jnp.concatenate([mine[of, :], peer[of, :]], axis=1)
        product = lax.dot_general(normed, weight, TN, preferred_element_type=f32)
        if place:
            total[...] += product
        else:
            total[...] = product
    keys[...] = total[pl.ds(0, tokens), :]
    for b in range(features // LANES):
        send[pl.ds(half + b * tokens, tokens), :] = total[pl.ds(tokens, tokens), lanes(b)].astype(bf16)


def finish(rows, ring, at, own, got, act, gain, inv, part, keys, out, turned, scaled):
    (tokens, width), z, h = act.shape, at[0], at[1]
    for place in range(ring):
        owner = lax.rem(z + place, ring)
        turned[owned(rows, 2 * owner + h), :] = own[block(rows, place), :]
        turned[owned(rows, 2 * owner + 1 - h), :] = got[block(rows, place), :]
    scale = inv[...]
    products = jnp.zeros((tokens, LANES), f32)
    for b in range(width // LANES):
        value = turned[lanes(b), :].astype(f32).T * (1.0 + gain[:, lanes(b)])
        scaled[:, lanes(b)] = value
        products = products + value * (act[:, lanes(b)].astype(f32) * scale)
    mean = jnp.sum(products, axis=1, keepdims=True) / width
    for b in range(width // LANES):
        unit = act[:, lanes(b)].astype(f32) * scale
        out[:, lanes(b)] = (scale * (scaled[:, lanes(b)] - unit * mean)).astype(bf16)
    for b in range(part.shape[1] // LANES):
        received = got[pl.ds(width // 2 + b * tokens, tokens), :].astype(f32)
        keys[:, lanes(b)] = (part[:, lanes(b)] + received).astype(bf16)


def local(activations, norm_gain, key_grad, numerator, push_weight, step_count):
    rows_in, grad_keys, numer_rows = activations[0], key_grad[0], numerator[0]
    tokens, width = rows_in.shape
    ring = lax.axis_size("z")
    turns = ring // 2
    at = jnp.stack([lax.axis_index("z"), lax.axis_index("h")]).astype(jnp.int32)
    rows, features = numer_rows.shape
    half, tail = width // 2, features // LANES * tokens
    work = 2 * tokens * width * features
    arc = ((turns * rows, features), bf16)

    mine, send, inv_rms, param, message = call(
        partial(normalise, rows, ring),
        [((half, tokens), bf16), ((half + tail, tokens), bf16), ((tokens, 1), f32),
         ((rows, features), bf16), ((rows + 16, features), bf16)],
        [pltpu.VMEM((width, tokens), bf16)], 10 * tokens * width, 6 * tokens * width,
    )(at, push_weight, rows_in, norm_gain, grad_keys, numer_rows)
    peer = sent(send, "h", 1)
    held = {0: param}

    def gather(step):
        held[ring - step] = sent(held[(ring - step + 1) % ring], "z", 1)
        if step < turns:
            held[step] = sent(held[step - 1], "z", -1)

    def newest(step):
        return [(ring - step) % ring] + ([step] if 0 < step < turns else [])

    def after_gather(step, *arrays):
        places = newest(step)
        *blocks, = together(*[held[p] for p in places], *arrays)
        held.update(zip(places, blocks))
        return blocks[len(places):]

    gather(1)
    peer, = after_gather(1, peer)
    part_up, part_down, both = call(
        partial(outer, rows, ring), [arc, arc, ((2 * tokens, features), bf16)], (), work, 2 * half * features,
    )(at, mine, peer, grad_keys)

    def part(place):
        array, i = (part_up, place) if place >= 0 else (part_down, place + turns)
        return lax.slice_in_dim(array, i * rows, (i + 1) * rows)

    up, down = part(turns - 1), part(-turns)

    def scatter(step, up, down):
        down = sent(down, "z", -1)
        if step < turns:
            up, down = sent(up, "z", 1), down + part(step - turns)
            up = up + part(turns - 1 - step) if step < turns - 1 else up
        return up, down

    lag = 1
    for step in range(lag + 1, turns + 1):
        gather(step)
        up, down = after_gather(step - 1, up, down)
        up, down = scatter(step - lag, up, down)
        if step > lag + 1:
            after_gather(step, *sums)
        sums = up, down
    own, send_back, part_keys = call(
        partial(project, rows, ring),
        [((half, tokens), bf16), ((half + tail, tokens), bf16), ((tokens, features), f32)],
        [pltpu.VMEM((2 * tokens, features), f32)], 2 * work, 2 * half * features,
    )(at, mine, peer, both, *(held[place] for place in range(ring)))
    send_back, message = together(send_back, message)
    back = sent(send_back, "h", 1)
    levels = lax.axis_size("gossip").bit_length() - 1
    got = lax.switch(
        lax.rem(step_count[0], levels), [partial(sent, axis="gossip", distance=2**level) for level in range(levels)], message
    )
    for step in range(turns - lag + 1, turns + 1):
        up, down = scatter(step, up, down)
    keys, input_grad = call(
        partial(finish, rows, ring),
        [((tokens, features), bf16), ((tokens, width), bf16)],
        [pltpu.VMEM((width, tokens), bf16), pltpu.VMEM((tokens, width), f32)], 10 * tokens * width, 8 * tokens * width,
    )(at, own, back, rows_in, norm_gain, inv_rms, part_keys)

    grad_rows = part(0).astype(f32) + up.astype(f32) + down.astype(f32)
    peer_numer, peer_weight = got[:rows].astype(f32), got[rows, :1].astype(f32)
    new_numerator = 0.5 * (numer_rows - learn_rate * grad_rows) + 0.5 * peer_numer
    new_weight = 0.5 * (push_weight + peer_weight)
    return (keys[None], input_grad[None], new_numerator[None], new_weight)


def solution(mesh):
    replicas, members = mesh.devices.shape
    split = Mesh(mesh.devices.reshape(replicas, members // 2, 2), ("gossip", "z", "h"))
    both = ("z", "h")
    return jax.shard_map(
        local,
        mesh=split,
        in_specs=(
            P("gossip", both, None),
            P("gossip", None),
            P("gossip", both, None),
            P("gossip", both, None),
            P("gossip"),
            P(),
        ),
        out_specs=(
            P("gossip", both, None),
            P("gossip", both, None),
            P("gossip", both, None),
            P("gossip"),
        ),
        check_vma=False,
    )
```

time: 461 us -> 176 us (0.38)
  waiting for transfers between devices: 394 us -> 24.1 us
  starting transfers between devices: 23 us -> 121 us
  matrix products: 17.3 us -> 0 us
  Pallas kernels: 0 us -> 13.7 us
  between operations: 16.6 us -> 4.29 us
    all_gather x2 -> x0, waiting for transfers between devices: 330 us -> none  [the longest x1 192 us: local(): full_weight = lax.all_gather(param, 'fsdp', axis=0, tiled=True)]
    ppermute x2 -> x33, starting transfers between devices: 4.99 us -> 121 us  [sent(): lax.ppermute(block, axis, [(i, (i + distance) % count) for i in range(cou...]
    all_to_all x1 -> x0, waiting for transfers between devices: 61.5 us -> none  [local(): lax.all_to_all(normed, 'fsdp', split_axis=1, concat_axis=0, tiled=True)]
    ppermute x2 -> x33, waiting for transfers between devices: 2.41 us -> 24.1 us  [sent(): lax.ppermute(block, axis, [(i, (i + distance) % count) for i in range(cou...]
    all_to_all x1 -> x0, starting transfers between devices: 17.9 us -> none  [local(): lax.all_to_all(normed, 'fsdp', split_axis=1, concat_axis=0, tiled=True)]
    dot_general x3 -> x0, matrix products: 17.3 us -> none  [the longest x1 6.24 us: local(): jnp.dot(normed, full_weight, preferred_element_type=jnp.float32)]
    pallas_call x0 -> x4, Pallas kernels: none -> 13.7 us  [run(): pl.pallas_call(body, out_shape=shapes, in_specs=[pl.BlockSpec(memory_spac...]
  transfers between devices with their start and end apart: 5 -> 33, of which waited for: 4 -> 8; matrix products, arithmetic and copies ran while one was open for 3% -> 3% of each run, Pallas kernels for 0% -> 4%
where the time goes in v1:
time: 176 us; the launch traced here: 174 us
  starting transfers between devices  121 us (69%)
  waiting for transfers between devices  24.1 us (14%)
  Pallas kernels  13.7 us (8%)
  local copies, waits for them, and re-layouts  7.1 us (4%)
  other arithmetic  4.35 us (2%)
  between operations  4.29 us (2%)
    ppermute x33, starting transfers between devices, sent(): lax.ppermute(block, axis, [(i, (i + distance) % count) for i in range(cou...  121 us
    ppermute x33, waiting for transfers between devices, sent(): lax.ppermute(block, axis, [(i, (i + distance) % count) for i in range(cou...  24.1 us
    pallas_call x4, Pallas kernels, run(): pl.pallas_call(body, out_shape=shapes, in_specs=[pl.BlockSpec(memory_spac...  13.7 us
    unnamed x26, local copies, waits for them, and re-layouts  5.78 us
  transfers between devices with their start and end apart: 33, of which 8 were waited for; matrix products, arithmetic and copies ran while one was open for 3% of the time, Pallas kernels for 4%

profile of v1, /device:TPU:24, one launch (start us, length us, event | category | flops | bytes accessed | tf_op | source)
XLA Modules:
  0.0 174.3 jit_solution(25956892123826704)
XLA Ops:
  7.5 4.9 %collective-permute-start.6 = (bf16[3328,128]{1,0:T(8,128)(2,1)S(1)}, bf16[3328,128]{1,0:T(8,128)(2,1)S(1)}, u32[]{:S(2)}, u32[]{:S(2)}) collective-permute-start(bf16[3328,128]{1,0:T(8,128)(2,1)S(1)} %get-tuple-element.72), channel_id=1, source_target_pairs={{0,1},{1,0},{2,3},{3,2},{4,5},{5,4},{6,7},{7,6},{8,9},{9,8},{10,11... | collective-permute-start | bytes 2555912 | tf_op jit(solution)/shard_map/ppermute | solution.py:20
  12.5 3.8 %collective-permute-start.4 = (bf16[144,1024]{1,0:T(8,128)(2,1)S(1)}, bf16[144,1024]{1,0:T(8,128)(2,1)S(1)}, u32[]{:S(2)}, u32[]{:S(2)}) collective-permute-start(bf16[144,1024]{1,0:T(8,128)(2,1)S(1)} %get-tuple-element.71.refs_0_), channel_id=1, source_target_pairs={{0,2},{2,4},{4,6},{6,8},{8,10},{10,12},{12,14},{14,16},{16,18},{18... | collective-permute-start | bytes 884744 | tf_op jit(solution)/shard_map/ppermute | solution.py:20
  16.3 9.5 %collective-permute-start.5 = (bf16[144,1024]{1,0:T(8,128)(2,1)S(1)}, bf16[144,1024]{1,0:T(8,128)(2,1)S(1)}, u32[]{:S(2)}, u32[]{:S(2)}) collective-permute-start(bf16[144,1024]{1,0:T(8,128)(2,1)S(1)} %get-tuple-element.71.refs_0_), channel_id=1, source_target_pairs={{0,30},{2,0},{4,2},{6,4},{8,6},{10,8},{12,10},{14,12},{16,14},{18,... | collective-permute-start | bytes 884744 | tf_op jit(solution)/shard_map/ppermute | solution.py:20
  25.8 4.8 %collective-permute-done.4.refs_15_ = bf16[144,1024]{1,0:T(8,128)(2,1)S(1)} collective-permute-done((bf16[144,1024]{1,0:T(8,128)(2,1)S(1)}, bf16[144,1024]{1,0:T(8,128)(2,1)S(1)}, u32[]{:S(2)}, u32[]{:S(2)}) %collective-permute-start.4) | collective-permute-done | bytes 294944 | tf_op jit(solution)/shard_map/ppermute | solution.py:20
  34.7 3.7 %collective-permute-start.7 = (bf16[144,1024]{1,0:T(8,128)(2,1)S(1)}, bf16[144,1024]{1,0:T(8,128)(2,1)S(1)}, u32[]{:S(2)}, u32[]{:S(2)}) collective-permute-start(bf16[144,1024]{1,0:T(8,128)(2,1)S(1)} %collective-permute-done.4.refs_15_), channel_id=1, source_target_pairs={{0,2},{2,4},{4,6},{6,8},{8,10},{10,12},{12,14},{14,16},{16,18},{18... | collective-permute-start | bytes 884744 | tf_op jit(solution)/shard_map/ppermute | solution.py:20
  38.4 9.5 %collective-permute-start.8 = (bf16[144,1024]{1,0:T(8,128)(2,1)S(1)}, bf16[144,1024]{1,0:T(8,128)(2,1)S(1)}, u32[]{:S(2)}, u32[]{:S(2)}) collective-permute-start(bf16[144,1024]{1,0:T(8,128)(2,1)S(1)} %collective-permute-done.5.refs_1_), channel_id=1, source_target_pairs={{0,30},{2,0},{4,2},{6,4},{8,6},{10,8},{12,10},{14,12},{16,14},{18,... | collective-permute-start | bytes 884744 | tf_op jit(solution)/shard_map/ppermute | solution.py:20
  47.9 3.9 %collective-permute-start.10 = (bf16[144,1024]{1,0:T(8,128)(2,1)S(1)}, bf16[144,1024]{1,0:T(8,128)(2,1)S(1)}, u32[]{:S(2)}, u32[]{:S(2)}) collective-permute-start(bf16[144,1024]{1,0:T(8,128)(2,1)S(1)} %slice.55), channel_id=1, source_target_pairs={{0,30},{2,0},{4,2},{6,4},{8,6},{10,8},{12,10},{14,12},{16,14},{18,... | collective-permute-start | bytes 884744 | tf_op jit(solution)/shard_map/ppermute | solution.py:20
  55.7 5.2 %collective-permute-start.12 = (bf16[144,1024]{1,0:T(8,128)(2,1)S(1)}, bf16[144,1024]{1,0:T(8,128)(2,1)S(1)}, u32[]{:S(2)}, u32[]{:S(2)}) collective-permute-start(bf16[144,1024]{1,0:T(8,128)(2,1)S(1)} %collective-permute-done.8.refs_2_), channel_id=1, source_target_pairs={{0,30},{2,0},{4,2},{6,4},{8,6},{10,8},{12,10},{14,12},{16,14},{18,... | collective-permute-start | bytes 884744 | tf_op jit(solution)/shard_map/ppermute | solution.py:20
  61.0 3.9 %collective-permute-done.9 = bf16[144,1024]{1,0:T(8,128)(2,1)S(1)} collective-permute-done((bf16[144,1024]{1,0:T(8,128)(2,1)S(1)}, bf16[144,1024]{1,0:T(8,128)(2,1)S(1)}, u32[]{:S(2)}, u32[]{:S(2)}) %collective-permute-start.9) | collective-permute-done | bytes 294944 | tf_op jit(solution)/shard_map/ppermute | solution.py:20
  66.9 3.9 %collective-permute-start.13 = (bf16[144,1024]{1,0:T(8,128)(2,1)S(1)}, bf16[144,1024]{1,0:T(8,128)(2,1)S(1)}, u32[]{:S(2)}, u32[]{:S(2)}) collective-permute-start(bf16[144,1024]{1,0:T(8,128)(2,1)S(1)} %slice_add_fusion.12), channel_id=1, source_target_pairs={{0,2},{2,4},{4,6},{6,8},{8,10},{10,12},{12,14},{14,16},{16,18},{18... | collective-permute-start | bytes 884744 | tf_op jit(solution)/shard_map/ppermute | solution.py:20
  72.8 5.1 %collective-permute-start.16 = (bf16[144,1024]{1,0:T(8,128)(2,1)S(1)}, bf16[144,1024]{1,0:T(8,128)(2,1)S(1)}, u32[]{:S(2)}, u32[]{:S(2)}) collective-permute-start(bf16[144,1024]{1,0:T(8,128)(2,1)S(1)} %collective-permute-done.12.refs_3_), channel_id=1, source_target_pairs={{0,30},{2,0},{4,2},{6,4},{8,6},{10,8},{12,10},{14,12},{16,14},{18,... | collective-permute-start | bytes 884744 | tf_op jit(solution)/shard_map/ppermute | solution.py:20
  78.3 2.4 %collective-permute-start.18 = (bf16[144,1024]{1,0:T(8,128)(2,1)S(1)}, bf16[144,1024]{1,0:T(8,128)(2,1)S(1)}, u32[]{:S(2)}, u32[]{:S(2)}) collective-permute-start(bf16[144,1024]{1,0:T(8,128)(2,1)S(1)} %slice_add_fusion.9), channel_id=1, source_target_pairs={{0,30},{2,0},{4,2},{6,4},{8,6},{10,8},{12,10},{14,12},{16,14},{18,... | collective-permute-start | bytes 884744 | tf_op jit(solution)/shard_map/ppermute | solution.py:20
  80.7 3.4 %collective-permute-start.17 = (bf16[144,1024]{1,0:T(8,128)(2,1)S(1)}, bf16[144,1024]{1,0:T(8,128)(2,1)S(1)}, u32[]{:S(2)}, u32[]{:S(2)}) collective-permute-start(bf16[144,1024]{1,0:T(8,128)(2,1)S(1)} %slice_add_fusion.10), channel_id=1, source_target_pairs={{0,2},{2,4},{4,6},{6,8},{8,10},{10,12},{12,14},{14,16},{16,18},{18... | collective-permute-start | bytes 884744 | tf_op jit(solution)/shard_map/ppermute | solution.py:20
  86.1 5.1 %collective-permute-start.20 = (bf16[144,1024]{1,0:T(8,128)(2,1)S(1)}, bf16[144,1024]{1,0:T(8,128)(2,1)S(1)}, u32[]{:S(2)}, u32[]{:S(2)}) collective-permute-start(bf16[144,1024]{1,0:T(8,128)(2,1)S(1)} %collective-permute-done.16.refs_4_), channel_id=1, source_target_pairs={{0,30},{2,0},{4,2},{6,4},{8,6},{10,8},{12,10},{14,12},{16,14},{18,... | collective-permute-start | bytes 884744 | tf_op jit(solution)/shard_map/ppermute | solution.py:20
  91.3 2.4 %collective-permute-start.22 = (bf16[144,1024]{1,0:T(8,128)(2,1)S(1)}, bf16[144,1024]{1,0:T(8,128)(2,1)S(1)}, u32[]{:S(2)}, u32[]{:S(2)}) collective-permute-start(bf16[144,1024]{1,0:T(8,128)(2,1)S(1)} %slice_add_fusion.7), channel_id=1, source_target_pairs={{0,30},{2,0},{4,2},{6,4},{8,6},{10,8},{12,10},{14,12},{16,14},{18,... | collective-permute-start | bytes 884744 | tf_op jit(solution)/shard_map/ppermute | solution.py:20
  93.8 3.4 %collective-permute-start.21 = (bf16[144,1024]{1,0:T(8,128)(2,1)S(1)}, bf16[144,1024]{1,0:T(8,128)(2,1)S(1)}, u32[]{:S(2)}, u32[]{:S(2)}) collective-permute-start(bf16[144,1024]{1,0:T(8,128)(2,1)S(1)} %slice_add_fusion.8), channel_id=1, source_target_pairs={{0,2},{2,4},{4,6},{6,8},{8,10},{10,12},{12,14},{14,16},{16,18},{18... | collective-permute-start | bytes 884744 | tf_op jit(solution)/shard_map/ppermute | solution.py:20
  99.1 5.1 %collective-permute-start.24 = (bf16[144,1024]{1,0:T(8,128)(2,1)S(1)}, bf16[144,1024]{1,0:T(8,128)(2,1)S(1)}, u32[]{:S(2)}, u32[]{:S(2)}) collective-permute-start(bf16[144,1024]{1,0:T(8,128)(2,1)S(1)} %collective-permute-done.20.refs_5_), channel_id=1, source_target_pairs={{0,30},{2,0},{4,2},{6,4},{8,6},{10,8},{12,10},{14,12},{16,14},{18,... | collective-permute-start | bytes 884744 | tf_op jit(solution)/shard_map/ppermute | solution.py:20
  104.4 2.6 %collective-permute-start.26 = (bf16[144,1024]{1,0:T(8,128)(2,1)S(1)}, bf16[144,1024]{1,0:T(8,128)(2,1)S(1)}, u32[]{:S(2)}, u32[]{:S(2)}) collective-permute-start(bf16[144,1024]{1,0:T(8,128)(2,1)S(1)} %slice_add_fusion.5), channel_id=1, source_target_pairs={{0,30},{2,0},{4,2},{6,4},{8,6},{10,8},{12,10},{14,12},{16,14},{18,... | collective-permute-start | bytes 884744 | tf_op jit(solution)/shard_map/ppermute | solution.py:20
  107.0 3.2 %collective-permute-start.25 = (bf16[144,1024]{1,0:T(8,128)(2,1)S(1)}, bf16[144,1024]{1,0:T(8,128)(2,1)S(1)}, u32[]{:S(2)}, u32[]{:S(2)}) collective-permute-start(bf16[144,1024]{1,0:T(8,128)(2,1)S(1)} %slice_add_fusion.6), channel_id=1, source_target_pairs={{0,2},{2,4},{4,6},{6,8},{8,10},{10,12},{12,14},{14,16},{16,18},{18... | collective-permute-start | bytes 884744 | tf_op jit(solution)/shard_map/ppermute | solution.py:20
  112.2 5.1 %collective-permute-start.28 = (bf16[144,1024]{1,0:T(8,128)(2,1)S(1)}, bf16[144,1024]{1,0:T(8,128)(2,1)S(1)}, u32[]{:S(2)}, u32[]{:S(2)}) collective-permute-start(bf16[144,1024]{1,0:T(8,128)(2,1)S(1)} %collective-permute-done.24.refs_6_), channel_id=1, source_target_pairs={{0,30},{2,0},{4,2},{6,4},{8,6},{10,8},{12,10},{14,12},{16,14},{18,... | collective-permute-start | bytes 884744 | tf_op jit(solution)/shard_map/ppermute | solution.py:20
  117.5 2.6 %collective-permute-start.30 = (bf16[144,1024]{1,0:T(8,128)(2,1)S(1)}, bf16[144,1024]{1,0:T(8,128)(2,1)S(1)}, u32[]{:S(2)}, u32[]{:S(2)}) collective-permute-start(bf16[144,1024]{1,0:T(8,128)(2,1)S(1)} %slice_add_fusion.3), channel_id=1, source_target_pairs={{0,30},{2,0},{4,2},{6,4},{8,6},{10,8},{12,10},{14,12},{16,14},{18,... | collective-permute-start | bytes 884744 | tf_op jit(solution)/shard_map/ppermute | solution.py:20
  120.1 3.2 %collective-permute-start.29 = (bf16[144,1024]{1,0:T(8,128)(2,1)S(1)}, bf16[144,1024]{1,0:T(8,128)(2,1)S(1)}, u32[]{:S(2)}, u32[]{:S(2)}) collective-permute-start(bf16[144,1024]{1,0:T(8,128)(2,1)S(1)} %slice_add_fusion.4), channel_id=1, source_target_pairs={{0,2},{2,4},{4,6},{6,8},{8,10},{10,12},{12,14},{14,16},{16,18},{18... | collective-permute-start | bytes 884744 | tf_op jit(solution)/shard_map/ppermute | solution.py:20
  126.1 3.8 %collective-permute-done.29 = bf16[144,1024]{1,0:T(8,128)(2,1)S(1)} collective-permute-done((bf16[144,1024]{1,0:T(8,128)(2,1)S(1)}, bf16[144,1024]{1,0:T(8,128)(2,1)S(1)}, u32[]{:S(2)}, u32[]{:S(2)}) %collective-permute-start.29) | collective-permute-done | bytes 294944 | tf_op jit(solution)/shard_map/ppermute | solution.py:20
  133.2 6.2 %shard_map.95 = (bf16[2304,128]{1,0:T(8,128)(2,1)S(1)}, bf16[3328,128]{1,0:T(8,128)(2,1)}, f32[128,1024]{1,0:T(8,128)S(1)}) custom-call(s32[2]{0:T(128)S(1)} %pad_add_fusion.at, bf16[2304,128]{1,0:T(8,128)(2,1)S(1)} %get-tuple-element.70.mine, bf16[3328,128]{1,0:T(8,128)(2,1)S(1)} %collective-permute-done.6.peer, ...), custom_call_target="tpu_custom_call" | custom-call | flops 2415919104 | bytes 4718592 | tf_op jit(solution)/shard_map/pallas_call | solution.py:36
  140.1 5.1 %collective-permute-start.32 = (bf16[3328,128]{1,0:T(8,128)(2,1)}, bf16[3328,128]{1,0:T(8,128)(2,1)}, u32[]{:S(2)}, u32[]{:S(2)}) collective-permute-start(bf16[3328,128]{1,0:T(8,128)(2,1)} %get-tuple-element.119), channel_id=1, source_target_pairs={{0,1},{1,0},{2,3},{3,2},{4,5},{5,4},{6,7},{7,6},{8,9},{9,8},{10,11... | collective-permute-start | bytes 2555912 | tf_op jit(solution)/shard_map/ppermute | solution.py:20
  145.2 3.4 %collective-permute-start.33 = (bf16[144,1024]{1,0:T(8,128)(2,1)}, bf16[144,1024]{1,0:T(8,128)(2,1)}, u32[]{:S(2)}, u32[]{:S(2)}) collective-permute-start(bf16[144,1024]{1,0:T(8,128)(2,1)} %slice_add_fusion.2), channel_id=1, source_target_pairs={{0,2},{2,4},{4,6},{6,8},{8,10},{10,12},{12,14},{14,16},{16,18},{18... | collective-permute-start | bytes 884744 | tf_op jit(solution)/shard_map/ppermute | solution.py:20
  149.3 3.7 %collective-permute-start.35 = (bf16[144,1024]{1,0:T(8,128)(2,1)}, bf16[144,1024]{1,0:T(8,128)(2,1)}, u32[]{:S(2)}, u32[]{:S(2)}) collective-permute-start(bf16[144,1024]{1,0:T(8,128)(2,1)} %slice_add_fusion), channel_id=1, source_target_pairs={{0,30},{2,0},{4,2},{6,4},{8,6},{10,8},{12,10},{14,12},{16,14},{18,... | collective-permute-start | bytes 884744 | tf_op jit(solution)/shard_map/ppermute | solution.py:20
  153.7 11.6 %conditional.1 = (bf16[160,1024]{1,0:T(8,128)(2,1)}) conditional(s32[]{:T(128)} %clamp.3, bf16[160,1024]{1,0:T(8,128)(2,1)} %get-tuple-element.126, bf16[160,1024]{1,0:T(8,128)(2,1)} %get-tuple-element.126, bf16[160,1024]{1,0:T(8,128)(2,1)} %get-tuple-element.126, bf16[160,1024]{1,0:T(8,128)(2,1)} %get-tuple-element.126), branch_computations={%region_0.0_spmd, %region_1.0_spmd, %region_2.0_spmd, %region_3.0_... | conditional | bytes 1310768 | solution.py:212
  153.7 2.5 %collective-permute-start.3 = (bf16[160,1024]{1,0:T(8,128)(2,1)}, bf16[160,1024]{1,0:T(8,128)(2,1)}, u32[]{:S(2)}, u32[]{:S(2)}) collective-permute-start(bf16[160,1024]{1,0:T(8,128)(2,1)} %param.3), channel_id=1, source_target_pairs={{0,256},{32,288},{64,320},{96,352},{128,384},{160,416},{192,448},{... | collective-permute-start | bytes 983048 | tf_op jit(solution)/shard_map/cond/branch_3_fun/ppermute | solution.py:20
  156.2 9.1 %collective-permute-done.3 = bf16[160,1024]{1,0:T(8,128)(2,1)} collective-permute-done((bf16[160,1024]{1,0:T(8,128)(2,1)}, bf16[160,1024]{1,0:T(8,128)(2,1)}, u32[]{:S(2)}, u32[]{:S(2)}) %collective-permute-start.3) | collective-permute-done | bytes 327712 | tf_op jit(solution)/shard_map/cond/branch_3_fun/ppermute | solution.py:20
  167.3 2.4 %multiply_bitcast_fusion = f32[1,144,1024]{2,1,0:T(8,128)} fusion(bf16[144,1024]{1,0:T(8,128)(2,1)} %collective-permute-done.35, bf16[144,1024]{1,0:T(8,128)(2,1)} %collective-permute-done.33, bf16[160,1024]{1,0:T(8,128)(2,1)} %get-tuple-element.127, bf16[1152,1024]{1,0:T(8,128)(2,1)S(1)} %get-tuple-element.77, f32[1,144,1024]{2,1,0:T(8,128)} %param.13), kind=kLoop, calls=%fused_computation | loop fusion | flops 1474560 | bytes 2359296 | tf_op jit(solution)/shard_map/broadcast_in_dim | solution.py:227
  169.7 3.5 %shard_map.96 = (bf16[128,1024]{1,0:T(8,128)(2,1)}, bf16[128,4608]{1,0:T(8,128)(2,1)}) custom-call(s32[2]{0:T(128)S(1)} %pad_add_fusion.at, bf16[2304,128]{1,0:T(8,128)(2,1)S(1)} %copy-done.4, bf16[3328,128]{1,0:T(8,128)(2,1)} %collective-permute-done.32.got, bf16[128,4608]{1,0:T(8,128)(2,1)S(1)} %bitcast.17, f32[1,4608]{1,0:T(1,128)S(1)} %copy-done.10, ...), custom_call_target="tpu_custom_call" | custom-call | flops 5898240 | bytes 4718592 | tf_op jit(solution)/shard_map/pallas_call | solution.py:36
  (83 shorter events, 33.4 us)
Async XLA Ops:
  7.5 24.2 %collective-permute-start.6 = (bf16[3328,128]{1,0:T(8,128)(2,1)S(1)}, bf16[3328,128]{1,0:T(8,128)(2,1)S(1)}, u32[]{:S(2)}, u32[]{:S(2)}) collective-permute-start(bf16[3328,128]{1,0:T(8,128)(2,1)S(1)} %get-tuple-element.72), channel_id=1, source_target_pairs={{0,1},{1,0},{2,3},{3,2},{4,5},{5,4},{6,7},{7,6},{8,9},{9,8},{10,11... | collective-permute-start | bytes 2555912 | tf_op jit(solution)/shard_map/ppermute | solution.py:20
  12.5 18.1 %collective-permute-start.4 = (bf16[144,1024]{1,0:T(8,128)(2,1)S(1)}, bf16[144,1024]{1,0:T(8,128)(2,1)S(1)}, u32[]{:S(2)}, u32[]{:S(2)}) collective-permute-start(bf16[144,1024]{1,0:T(8,128)(2,1)S(1)} %get-tuple-element.71.refs_0_), channel_id=1, source_target_pairs={{0,2},{2,4},{4,6},{6,8},{8,10},{10,12},{12,14},{14,16},{16,18},{18... | collective-permute-start | bytes 884744 | tf_op jit(solution)/shard_map/ppermute | solution.py:20
  16.3 15.5 %collective-permute-start.5 = (bf16[144,1024]{1,0:T(8,128)(2,1)S(1)}, bf16[144,1024]{1,0:T(8,128)(2,1)S(1)}, u32[]{:S(2)}, u32[]{:S(2)}) collective-permute-start(bf16[144,1024]{1,0:T(8,128)(2,1)S(1)} %get-tuple-element.71.refs_0_), channel_id=1, source_target_pairs={{0,30},{2,0},{4,2},{6,4},{8,6},{10,8},{12,10},{14,12},{16,14},{18,... | collective-permute-start | bytes 884744 | tf_op jit(solution)/shard_map/ppermute | solution.py:20
  34.7 19.0 %collective-permute-start.7 = (bf16[144,1024]{1,0:T(8,128)(2,1)S(1)}, bf16[144,1024]{1,0:T(8,128)(2,1)S(1)}, u32[]{:S(2)}, u32[]{:S(2)}) collective-permute-start(bf16[144,1024]{1,0:T(8,128)(2,1)S(1)} %collective-permute-done.4.refs_15_), channel_id=1, source_target_pairs={{0,2},{2,4},{4,6},{6,8},{8,10},{10,12},{12,14},{14,16},{16,18},{18... | collective-permute-start | bytes 884744 | tf_op jit(solution)/shard_map/ppermute | solution.py:20
  38.4 17.3 %collective-permute-start.8 = (bf16[144,1024]{1,0:T(8,128)(2,1)S(1)}, bf16[144,1024]{1,0:T(8,128)(2,1)S(1)}, u32[]{:S(2)}, u32[]{:S(2)}) collective-permute-start(bf16[144,1024]{1,0:T(8,128)(2,1)S(1)} %collective-permute-done.5.refs_1_), channel_id=1, source_target_pairs={{0,30},{2,0},{4,2},{6,4},{8,6},{10,8},{12,10},{14,12},{16,14},{18,... | collective-permute-start | bytes 884744 | tf_op jit(solution)/shard_map/ppermute | solution.py:20
  47.9 13.0 %collective-permute-start.10 = (bf16[144,1024]{1,0:T(8,128)(2,1)S(1)}, bf16[144,1024]{1,0:T(8,128)(2,1)S(1)}, u32[]{:S(2)}, u32[]{:S(2)}) collective-permute-start(bf16[144,1024]{1,0:T(8,128)(2,1)S(1)} %slice.55), channel_id=1, source_target_pairs={{0,30},{2,0},{4,2},{6,4},{8,6},{10,8},{12,10},{14,12},{16,14},{18,... | collective-permute-start | bytes 884744 | tf_op jit(solution)/shard_map/ppermute | solution.py:20
  51.8 13.1 %collective-permute-start.9 = (bf16[144,1024]{1,0:T(8,128)(2,1)S(1)}, bf16[144,1024]{1,0:T(8,128)(2,1)S(1)}, u32[]{:S(2)}, u32[]{:S(2)}) collective-permute-start(bf16[144,1024]{1,0:T(8,128)(2,1)S(1)} %slice.54), channel_id=1, source_target_pairs={{0,2},{2,4},{4,6},{6,8},{8,10},{10,12},{12,14},{14,16},{16,18},{18... | collective-permute-start | bytes 884744 | tf_op jit(solution)/shard_map/ppermute | solution.py:20
  53.8 17.0 %collective-permute-start.11 = (bf16[144,1024]{1,0:T(8,128)(2,1)S(1)}, bf16[144,1024]{1,0:T(8,128)(2,1)S(1)}, u32[]{:S(2)}, u32[]{:S(2)}) collective-permute-start(bf16[144,1024]{1,0:T(8,128)(2,1)S(1)} %collective-permute-done.7.refs_14_), channel_id=1, source_target_pairs={{0,2},{2,4},{4,6},{6,8},{8,10},{10,12},{12,14},{14,16},{16,18},{18... | collective-permute-start | bytes 884744 | tf_op jit(solution)/shard_map/ppermute | solution.py:20
  55.7 15.1 %collective-permute-start.12 = (bf16[144,1024]{1,0:T(8,128)(2,1)S(1)}, bf16[144,1024]{1,0:T(8,128)(2,1)S(1)}, u32[]{:S(2)}, u32[]{:S(2)}) collective-permute-start(bf16[144,1024]{1,0:T(8,128)(2,1)S(1)} %collective-permute-done.8.refs_2_), channel_id=1, source_target_pairs={{0,30},{2,0},{4,2},{6,4},{8,6},{10,8},{12,10},{14,12},{16,14},{18,... | collective-permute-start | bytes 884744 | tf_op jit(solution)/shard_map/ppermute | solution.py:20
  64.9 13.0 %collective-permute-start.14 = (bf16[144,1024]{1,0:T(8,128)(2,1)S(1)}, bf16[144,1024]{1,0:T(8,128)(2,1)S(1)}, u32[]{:S(2)}, u32[]{:S(2)}) collective-permute-start(bf16[144,1024]{1,0:T(8,128)(2,1)S(1)} %slice_add_fusion.11), channel_id=1, source_target_pairs={{0,30},{2,0},{4,2},{6,4},{8,6},{10,8},{12,10},{14,12},{16,14},{18,... | collective-permute-start | bytes 884744 | tf_op jit(solution)/shard_map/ppermute | solution.py:20
  66.9 11.4 %collective-permute-start.13 = (bf16[144,1024]{1,0:T(8,128)(2,1)S(1)}, bf16[144,1024]{1,0:T(8,128)(2,1)S(1)}, u32[]{:S(2)}, u32[]{:S(2)}) collective-permute-start(bf16[144,1024]{1,0:T(8,128)(2,1)S(1)} %slice_add_fusion.12), channel_id=1, source_target_pairs={{0,2},{2,4},{4,6},{6,8},{8,10},{10,12},{12,14},{14,16},{16,18},{18... | collective-permute-start | bytes 884744 | tf_op jit(solution)/shard_map/ppermute | solution.py:20
  70.8 13.3 %collective-permute-start.15 = (bf16[144,1024]{1,0:T(8,128)(2,1)S(1)}, bf16[144,1024]{1,0:T(8,128)(2,1)S(1)}, u32[]{:S(2)}, u32[]{:S(2)}) collective-permute-start(bf16[144,1024]{1,0:T(8,128)(2,1)S(1)} %collective-permute-done.11.refs_13_), channel_id=1, source_target_pairs={{0,2},{2,4},{4,6},{6,8},{8,10},{10,12},{12,14},{14,16},{16,18},{18... | collective-permute-start | bytes 884744 | tf_op jit(solution)/shard_map/ppermute | solution.py:20
  72.8 11.4 %collective-permute-start.16 = (bf16[144,1024]{1,0:T(8,128)(2,1)S(1)}, bf16[144,1024]{1,0:T(8,128)(2,1)S(1)}, u32[]{:S(2)}, u32[]{:S(2)}) collective-permute-start(bf16[144,1024]{1,0:T(8,128)(2,1)S(1)} %collective-permute-done.12.refs_3_), channel_id=1, source_target_pairs={{0,30},{2,0},{4,2},{6,4},{8,6},{10,8},{12,10},{14,12},{16,14},{18,... | collective-permute-start | bytes 884744 | tf_op jit(solution)/shard_map/ppermute | solution.py:20
  78.3 13.0 %collective-permute-start.18 = (bf16[144,1024]{1,0:T(8,128)(2,1)S(1)}, bf16[144,1024]{1,0:T(8,128)(2,1)S(1)}, u32[]{:S(2)}, u32[]{:S(2)}) collective-permute-start(bf16[144,1024]{1,0:T(8,128)(2,1)S(1)} %slice_add_fusion.9), channel_id=1, source_target_pairs={{0,30},{2,0},{4,2},{6,4},{8,6},{10,8},{12,10},{14,12},{16,14},{18,... | collective-permute-start | bytes 884744 | tf_op jit(solution)/shard_map/ppermute | solution.py:20
  80.7 10.6 %collective-permute-start.17 = (bf16[144,1024]{1,0:T(8,128)(2,1)S(1)}, bf16[144,1024]{1,0:T(8,128)(2,1)S(1)}, u32[]{:S(2)}, u32[]{:S(2)}) collective-permute-start(bf16[144,1024]{1,0:T(8,128)(2,1)S(1)} %slice_add_fusion.10), channel_id=1, source_target_pairs={{0,2},{2,4},{4,6},{6,8},{8,10},{10,12},{12,14},{14,16},{16,18},{18... | collective-permute-start | bytes 884744 | tf_op jit(solution)/shard_map/ppermute | solution.py:20
  84.2 13.0 %collective-permute-start.19 = (bf16[144,1024]{1,0:T(8,128)(2,1)S(1)}, bf16[144,1024]{1,0:T(8,128)(2,1)S(1)}, u32[]{:S(2)}, u32[]{:S(2)}) collective-permute-start(bf16[144,1024]{1,0:T(8,128)(2,1)S(1)} %collective-permute-done.15.refs_12_), channel_id=1, source_target_pairs={{0,2},{2,4},{4,6},{6,8},{8,10},{10,12},{12,14},{14,16},{16,18},{18... | collective-permute-start | bytes 884744 | tf_op jit(solution)/shard_map/ppermute | solution.py:20
  86.1 11.1 %collective-permute-start.20 = (bf16[144,1024]{1,0:T(8,128)(2,1)S(1)}, bf16[144,1024]{1,0:T(8,128)(2,1)S(1)}, u32[]{:S(2)}, u32[]{:S(2)}) collective-permute-start(bf16[144,1024]{1,0:T(8,128)(2,1)S(1)} %collective-permute-done.16.refs_4_), channel_id=1, source_target_pairs={{0,30},{2,0},{4,2},{6,4},{8,6},{10,8},{12,10},{14,12},{16,14},{18,... | collective-permute-start | bytes 884744 | tf_op jit(solution)/shard_map/ppermute | solution.py:20
  91.3 13.0 %collective-permute-start.22 = (bf16[144,1024]{1,0:T(8,128)(2,1)S(1)}, bf16[144,1024]{1,0:T(8,128)(2,1)S(1)}, u32[]{:S(2)}, u32[]{:S(2)}) collective-permute-start(bf16[144,1024]{1,0:T(8,128)(2,1)S(1)} %slice_add_fusion.7), channel_id=1, source_target_pairs={{0,30},{2,0},{4,2},{6,4},{8,6},{10,8},{12,10},{14,12},{16,14},{18,... | collective-permute-start | bytes 884744 | tf_op jit(solution)/shard_map/ppermute | solution.py:20
  93.8 10.6 %collective-permute-start.21 = (bf16[144,1024]{1,0:T(8,128)(2,1)S(1)}, bf16[144,1024]{1,0:T(8,128)(2,1)S(1)}, u32[]{:S(2)}, u32[]{:S(2)}) collective-permute-start(bf16[144,1024]{1,0:T(8,128)(2,1)S(1)} %slice_add_fusion.8), channel_id=1, source_target_pairs={{0,2},{2,4},{4,6},{6,8},{8,10},{10,12},{12,14},{14,16},{16,18},{18... | collective-permute-start | bytes 884744 | tf_op jit(solution)/shard_map/ppermute | solution.py:20
  97.2 13.0 %collective-permute-start.23 = (bf16[144,1024]{1,0:T(8,128)(2,1)S(1)}, bf16[144,1024]{1,0:T(8,128)(2,1)S(1)}, u32[]{:S(2)}, u32[]{:S(2)}) collective-permute-start(bf16[144,1024]{1,0:T(8,128)(2,1)S(1)} %collective-permute-done.19.refs_11_), channel_id=1, source_target_pairs={{0,2},{2,4},{4,6},{6,8},{8,10},{10,12},{12,14},{14,16},{16,18},{18... | collective-permute-start | bytes 884744 | tf_op jit(solution)/shard_map/ppermute | solution.py:20
  99.1 11.1 %collective-permute-start.24 = (bf16[144,1024]{1,0:T(8,128)(2,1)S(1)}, bf16[144,1024]{1,0:T(8,128)(2,1)S(1)}, u32[]{:S(2)}, u32[]{:S(2)}) collective-permute-start(bf16[144,1024]{1,0:T(8,128)(2,1)S(1)} %collective-permute-done.20.refs_5_), channel_id=1, source_target_pairs={{0,30},{2,0},{4,2},{6,4},{8,6},{10,8},{12,10},{14,12},{16,14},{18,... | collective-permute-start | bytes 884744 | tf_op jit(solution)/shard_map/ppermute | solution.py:20
  104.4 13.0 %collective-permute-start.26 = (bf16[144,1024]{1,0:T(8,128)(2,1)S(1)}, bf16[144,1024]{1,0:T(8,128)(2,1)S(1)}, u32[]{:S(2)}, u32[]{:S(2)}) collective-permute-start(bf16[144,1024]{1,0:T(8,128)(2,1)S(1)} %slice_add_fusion.5), channel_id=1, source_target_pairs={{0,30},{2,0},{4,2},{6,4},{8,6},{10,8},{12,10},{14,12},{16,14},{18,... | collective-permute-start | bytes 884744 | tf_op jit(solution)/shard_map/ppermute | solution.py:20
  107.0 10.4 %collective-permute-start.25 = (bf16[144,1024]{1,0:T(8,128)(2,1)S(1)}, bf16[144,1024]{1,0:T(8,128)(2,1)S(1)}, u32[]{:S(2)}, u32[]{:S(2)}) collective-permute-start(bf16[144,1024]{1,0:T(8,128)(2,1)S(1)} %slice_add_fusion.6), channel_id=1, source_target_pairs={{0,2},{2,4},{4,6},{6,8},{8,10},{10,12},{12,14},{14,16},{16,18},{18... | collective-permute-start | bytes 884744 | tf_op jit(solution)/shard_map/ppermute | solution.py:20
  110.3 13.0 %collective-permute-start.27 = (bf16[144,1024]{1,0:T(8,128)(2,1)S(1)}, bf16[144,1024]{1,0:T(8,128)(2,1)S(1)}, u32[]{:S(2)}, u32[]{:S(2)}) collective-permute-start(bf16[144,1024]{1,0:T(8,128)(2,1)S(1)} %collective-permute-done.23.refs_10_), channel_id=1, source_target_pairs={{0,2},{2,4},{4,6},{6,8},{8,10},{10,12},{12,14},{14,16},{16,18},{18... | collective-permute-start | bytes 884744 | tf_op jit(solution)/shard_map/ppermute | solution.py:20
  112.2 11.1 %collective-permute-start.28 = (bf16[144,1024]{1,0:T(8,128)(2,1)S(1)}, bf16[144,1024]{1,0:T(8,128)(2,1)S(1)}, u32[]{:S(2)}, u32[]{:S(2)}) collective-permute-start(bf16[144,1024]{1,0:T(8,128)(2,1)S(1)} %collective-permute-done.24.refs_6_), channel_id=1, source_target_pairs={{0,30},{2,0},{4,2},{6,4},{8,6},{10,8},{12,10},{14,12},{16,14},{18,... | collective-permute-start | bytes 884744 | tf_op jit(solution)/shard_map/ppermute | solution.py:20
  120.1 9.8 %collective-permute-start.29 = (bf16[144,1024]{1,0:T(8,128)(2,1)S(1)}, bf16[144,1024]{1,0:T(8,128)(2,1)S(1)}, u32[]{:S(2)}, u32[]{:S(2)}) collective-permute-start(bf16[144,1024]{1,0:T(8,128)(2,1)S(1)} %slice_add_fusion.4), channel_id=1, source_target_pairs={{0,2},{2,4},{4,6},{6,8},{8,10},{10,12},{12,14},{14,16},{16,18},{18... | collective-permute-start | bytes 884744 | tf_op jit(solution)/shard_map/ppermute | solution.py:20
  123.3 9.8 %collective-permute-start.31 = (bf16[144,1024]{1,0:T(8,128)(2,1)S(1)}, bf16[144,1024]{1,0:T(8,128)(2,1)S(1)}, u32[]{:S(2)}, u32[]{:S(2)}) collective-permute-start(bf16[144,1024]{1,0:T(8,128)(2,1)S(1)} %collective-permute-done.27.refs_9_), channel_id=1, source_target_pairs={{0,2},{2,4},{4,6},{6,8},{8,10},{10,12},{12,14},{14,16},{16,18},{18... | collective-permute-start | bytes 884744 | tf_op jit(solution)/shard_map/ppermute | solution.py:20
  130.7 17.9 %collective-permute-start.34 = (bf16[144,1024]{1,0:T(8,128)(2,1)S(1)}, bf16[144,1024]{1,0:T(8,128)(2,1)S(1)}, u32[]{:S(2)}, u32[]{:S(2)}) collective-permute-start(bf16[144,1024]{1,0:T(8,128)(2,1)S(1)} %slice_add_fusion.1), channel_id=1, source_target_pairs={{0,30},{2,0},{4,2},{6,4},{8,6},{10,8},{12,10},{14,12},{16,14},{18,... | collective-permute-start | bytes 884744 | tf_op jit(solution)/shard_map/ppermute | solution.py:20
  140.1 29.5 %collective-permute-start.32 = (bf16[3328,128]{1,0:T(8,128)(2,1)}, bf16[3328,128]{1,0:T(8,128)(2,1)}, u32[]{:S(2)}, u32[]{:S(2)}) collective-permute-start(bf16[3328,128]{1,0:T(8,128)(2,1)} %get-tuple-element.119), channel_id=1, source_target_pairs={{0,1},{1,0},{2,3},{3,2},{4,5},{5,4},{6,7},{7,6},{8,9},{9,8},{10,11... | collective-permute-start | bytes 2555912 | tf_op jit(solution)/shard_map/ppermute | solution.py:20
  145.2 22.0 %collective-permute-start.33 = (bf16[144,1024]{1,0:T(8,128)(2,1)}, bf16[144,1024]{1,0:T(8,128)(2,1)}, u32[]{:S(2)}, u32[]{:S(2)}) collective-permute-start(bf16[144,1024]{1,0:T(8,128)(2,1)} %slice_add_fusion.2), channel_id=1, source_target_pairs={{0,2},{2,4},{4,6},{6,8},{8,10},{10,12},{12,14},{14,16},{16,18},{18... | collective-permute-start | bytes 884744 | tf_op jit(solution)/shard_map/ppermute | solution.py:20
  149.3 17.9 %collective-permute-start.35 = (bf16[144,1024]{1,0:T(8,128)(2,1)}, bf16[144,1024]{1,0:T(8,128)(2,1)}, u32[]{:S(2)}, u32[]{:S(2)}) collective-permute-start(bf16[144,1024]{1,0:T(8,128)(2,1)} %slice_add_fusion), channel_id=1, source_target_pairs={{0,30},{2,0},{4,2},{6,4},{8,6},{10,8},{12,10},{14,12},{16,14},{18,... | collective-permute-start | bytes 884744 | tf_op jit(solution)/shard_map/ppermute | solution.py:20
  153.7 11.6 %collective-permute-start.3 = (bf16[160,1024]{1,0:T(8,128)(2,1)}, bf16[160,1024]{1,0:T(8,128)(2,1)}, u32[]{:S(2)}, u32[]{:S(2)}) collective-permute-start(bf16[160,1024]{1,0:T(8,128)(2,1)} %param.3), channel_id=1, source_target_pairs={{0,256},{32,288},{64,320},{96,352},{128,384},{160,416},{192,448},{... | collective-permute-start | bytes 983048 | tf_op jit(solution)/shard_map/cond/branch_3_fun/ppermute | solution.py:20
  (14 other events, 97.6 us)

commit v2 on v1

--- a/solution.py
+++ b/solution.py
@@ -175,7 +175,11 @@
         return blocks[len(places):]
 
     gather(1)
-    peer, = after_gather(1, peer)
+    levels = lax.axis_size("gossip").bit_length() - 1
+    got = lax.switch(
+        lax.rem(step_count[0], levels), [partial(sent, axis="gossip", distance=2**level) for level in range(levels)], message
+    )
+    peer, got = after_gather(1, peer, got)
     part_up, part_down, both = call(
         partial(outer, rows, ring), [arc, arc, ((2 * tokens, features), bf16)], (), work, 2 * half * features,
     )(at, mine, peer, grad_keys)
@@ -206,12 +210,7 @@
         [((half, tokens), bf16), ((half + tail, tokens), bf16), ((tokens, features), f32)],
         [pltpu.VMEM((2 * tokens, features), f32)], 2 * work, 2 * half * features,
     )(at, mine, peer, both, *(held[place] for place in range(ring)))
-    send_back, message = together(send_back, message)
     back = sent(send_back, "h", 1)
-    levels = lax.axis_size("gossip").bit_length() - 1
-    got = lax.switch(
-        lax.rem(step_count[0], levels), [partial(sent, axis="gossip", distance=2**level) for level in range(levels)], message
-    )
     for step in range(turns - lag + 1, turns + 1):
         up, down = scatter(step, up, down)
     keys, input_grad = call(

time: 176 us -> 170 us (0.966)
  the two profiles are of different devices: /device:TPU:24 before, /device:TPU:2 now
where the time goes in v2:
time: 170 us
  starting transfers between devices  118 us (69%)
  waiting for transfers between devices  26.4 us (16%)
  Pallas kernels  12.2 us (7%)
  local copies, waits for them, and re-layouts  6.19 us (4%)
  between operations  4.3 us (3%)
  other arithmetic  2.5 us (1%)
    ppermute x33, starting transfers between devices, sent(): lax.ppermute(block, axis, [(i, (i + distance) % count) for i in range(cou...  118 us
    ppermute x33, waiting for transfers between devices, sent(): lax.ppermute(block, axis, [(i, (i + distance) % count) for i in range(cou...  26.4 us
    pallas_call x4, Pallas kernels, run(): pl.pallas_call(body, out_shape=shapes, in_specs=[pl.BlockSpec(memory_spac...  12.2 us
    unnamed x16, local copies, waits for them, and re-layouts  4.97 us
  transfers between devices with their start and end apart: 33, of which 9 were waited for; matrix products, arithmetic and copies ran while one was open for 2% of the time, Pallas kernels for 3%

profile of v2, /device:TPU:2, one launch (start us, length us, event | category | flops | bytes accessed | tf_op | source)
XLA Modules:
  0.0 169.5 jit_solution(3172794264164435778)
XLA Ops:
  5.4 2.2 %shard_map.93 = (bf16[2304,128]{1,0:T(8,128)(2,1)S(1)}, bf16[3328,128]{1,0:T(8,128)(2,1)S(1)}, f32[128,1]{1,0:T(8,128)S(1)}, bf16[144,1024]{1,0:T(8,128)(2,1)S(1)}, bf16[160,1024]{1,0:T(8,128)(2,1)}) custom-call(s32[2]{0:T(128)S(1)} %pad_add_fusion.at, f32[1]{0:T(128)S(6)} %copy.14.push, bf16[128,4608]{1,0:T(8,128)(2,1)S(1)} %bitcast.16, ...), custom_call_target="tpu_custom_call" | custom-call | flops 5898240 | bytes 3538944 | tf_op jit(solution)/shard_map/pallas_call | solution.py:36
  7.5 4.0 %collective-permute-start.6 = (bf16[3328,128]{1,0:T(8,128)(2,1)S(1)}, bf16[3328,128]{1,0:T(8,128)(2,1)S(1)}, u32[]{:S(2)}, u32[]{:S(2)}) collective-permute-start(bf16[3328,128]{1,0:T(8,128)(2,1)S(1)} %get-tuple-element.71), channel_id=1, source_target_pairs={{0,1},{1,0},{2,3},{3,2},{4,5},{5,4},{6,7},{7,6},{8,9},{9,8},{10,11... | collective-permute-start | bytes 2555912 | tf_op jit(solution)/shard_map/ppermute | solution.py:20
  11.6 3.8 %collective-permute-start.4 = (bf16[144,1024]{1,0:T(8,128)(2,1)S(1)}, bf16[144,1024]{1,0:T(8,128)(2,1)S(1)}, u32[]{:S(2)}, u32[]{:S(2)}) collective-permute-start(bf16[144,1024]{1,0:T(8,128)(2,1)S(1)} %get-tuple-element.70.refs_0_), channel_id=1, source_target_pairs={{0,2},{2,4},{4,6},{6,8},{8,10},{10,12},{12,14},{14,16},{16,18},{18... | collective-permute-start | bytes 884744 | tf_op jit(solution)/shard_map/ppermute | solution.py:20
  15.4 9.5 %collective-permute-start.5 = (bf16[144,1024]{1,0:T(8,128)(2,1)S(1)}, bf16[144,1024]{1,0:T(8,128)(2,1)S(1)}, u32[]{:S(2)}, u32[]{:S(2)}) collective-permute-start(bf16[144,1024]{1,0:T(8,128)(2,1)S(1)} %get-tuple-element.70.refs_0_), channel_id=1, source_target_pairs={{0,30},{2,0},{4,2},{6,4},{8,6},{10,8},{12,10},{14,12},{16,14},{18,... | collective-permute-start | bytes 884744 | tf_op jit(solution)/shard_map/ppermute | solution.py:20
  25.6 15.7 %conditional.1 = (bf16[160,1024]{1,0:T(8,128)(2,1)}) conditional(s32[]{:T(128)} %clamp.3, bf16[160,1024]{1,0:T(8,128)(2,1)} %get-tuple-element.72, bf16[160,1024]{1,0:T(8,128)(2,1)} %get-tuple-element.72, bf16[160,1024]{1,0:T(8,128)(2,1)} %get-tuple-element.72, bf16[160,1024]{1,0:T(8,128)(2,1)} %get-tuple-element.72), branch_computations={%region_0.0_spmd, %region_1.0_spmd, %region_2.0_spmd, %region_3.0_... | conditional | bytes 1310768 | solution.py:179
  25.6 3.5 %collective-permute-start.1 = (bf16[160,1024]{1,0:T(8,128)(2,1)}, bf16[160,1024]{1,0:T(8,128)(2,1)}, u32[]{:S(2)}, u32[]{:S(2)}) collective-permute-start(bf16[160,1024]{1,0:T(8,128)(2,1)} %param.1), channel_id=1, source_target_pairs={{0,64},{32,96},{64,128},{96,160},{128,192},{160,224},{192,256},{22... | collective-permute-start | bytes 983048 | tf_op jit(solution)/shard_map/cond/branch_1_fun/ppermute | solution.py:20
  29.1 12.1 %collective-permute-done.1 = bf16[160,1024]{1,0:T(8,128)(2,1)} collective-permute-done((bf16[160,1024]{1,0:T(8,128)(2,1)}, bf16[160,1024]{1,0:T(8,128)(2,1)}, u32[]{:S(2)}, u32[]{:S(2)}) %collective-permute-start.1) | collective-permute-done | bytes 327712 | tf_op jit(solution)/shard_map/cond/branch_1_fun/ppermute | solution.py:20
  44.2 3.8 %collective-permute-start.7 = (bf16[144,1024]{1,0:T(8,128)(2,1)S(1)}, bf16[144,1024]{1,0:T(8,128)(2,1)S(1)}, u32[]{:S(2)}, u32[]{:S(2)}) collective-permute-start(bf16[144,1024]{1,0:T(8,128)(2,1)S(1)} %collective-permute-done.4.refs_15_), channel_id=1, source_target_pairs={{0,2},{2,4},{4,6},{6,8},{8,10},{10,12},{12,14},{14,16},{16,18},{18... | collective-permute-start | bytes 884744 | tf_op jit(solution)/shard_map/ppermute | solution.py:20
  48.0 9.5 %collective-permute-start.8 = (bf16[144,1024]{1,0:T(8,128)(2,1)S(1)}, bf16[144,1024]{1,0:T(8,128)(2,1)S(1)}, u32[]{:S(2)}, u32[]{:S(2)}) collective-permute-start(bf16[144,1024]{1,0:T(8,128)(2,1)S(1)} %collective-permute-done.5.refs_1_), channel_id=1, source_target_pairs={{0,30},{2,0},{4,2},{6,4},{8,6},{10,8},{12,10},{14,12},{16,14},{18,... | collective-permute-start | bytes 884744 | tf_op jit(solution)/shard_map/ppermute | solution.py:20
  57.5 3.9 %collective-permute-start.10 = (bf16[144,1024]{1,0:T(8,128)(2,1)S(1)}, bf16[144,1024]{1,0:T(8,128)(2,1)S(1)}, u32[]{:S(2)}, u32[]{:S(2)}) collective-permute-start(bf16[144,1024]{1,0:T(8,128)(2,1)S(1)} %slice.55), channel_id=1, source_target_pairs={{0,30},{2,0},{4,2},{6,4},{8,6},{10,8},{12,10},{14,12},{16,14},{18,... | collective-permute-start | bytes 884744 | tf_op jit(solution)/shard_map/ppermute | solution.py:20
  65.3 5.2 %collective-permute-start.12 = (bf16[144,1024]{1,0:T(8,128)(2,1)S(1)}, bf16[144,1024]{1,0:T(8,128)(2,1)S(1)}, u32[]{:S(2)}, u32[]{:S(2)}) collective-permute-start(bf16[144,1024]{1,0:T(8,128)(2,1)S(1)} %collective-permute-done.8.refs_2_), channel_id=1, source_target_pairs={{0,30},{2,0},{4,2},{6,4},{8,6},{10,8},{12,10},{14,12},{16,14},{18,... | collective-permute-start | bytes 884744 | tf_op jit(solution)/shard_map/ppermute | solution.py:20
  70.6 3.9 %collective-permute-done.9 = bf16[144,1024]{1,0:T(8,128)(2,1)S(1)} collective-permute-done((bf16[144,1024]{1,0:T(8,128)(2,1)S(1)}, bf16[144,1024]{1,0:T(8,128)(2,1)S(1)}, u32[]{:S(2)}, u32[]{:S(2)}) %collective-permute-start.9) | collective-permute-done | bytes 294944 | tf_op jit(solution)/shard_map/ppermute | solution.py:20
  76.5 3.9 %collective-permute-start.13 = (bf16[144,1024]{1,0:T(8,128)(2,1)S(1)}, bf16[144,1024]{1,0:T(8,128)(2,1)S(1)}, u32[]{:S(2)}, u32[]{:S(2)}) collective-permute-start(bf16[144,1024]{1,0:T(8,128)(2,1)S(1)} %slice_add_fusion.12), channel_id=1, source_target_pairs={{0,2},{2,4},{4,6},{6,8},{8,10},{10,12},{12,14},{14,16},{16,18},{18... | collective-permute-start | bytes 884744 | tf_op jit(solution)/shard_map/ppermute | solution.py:20
  82.4 5.1 %collective-permute-start.16 = (bf16[144,1024]{1,0:T(8,128)(2,1)S(1)}, bf16[144,1024]{1,0:T(8,128)(2,1)S(1)}, u32[]{:S(2)}, u32[]{:S(2)}) collective-permute-start(bf16[144,1024]{1,0:T(8,128)(2,1)S(1)} %collective-permute-done.12.refs_3_), channel_id=1, source_target_pairs={{0,30},{2,0},{4,2},{6,4},{8,6},{10,8},{12,10},{14,12},{16,14},{18,... | collective-permute-start | bytes 884744 | tf_op jit(solution)/shard_map/ppermute | solution.py:20
  87.9 2.4 %collective-permute-start.18 = (bf16[144,1024]{1,0:T(8,128)(2,1)S(1)}, bf16[144,1024]{1,0:T(8,128)(2,1)S(1)}, u32[]{:S(2)}, u32[]{:S(2)}) collective-permute-start(bf16[144,1024]{1,0:T(8,128)(2,1)S(1)} %slice_add_fusion.9), channel_id=1, source_target_pairs={{0,30},{2,0},{4,2},{6,4},{8,6},{10,8},{12,10},{14,12},{16,14},{18,... | collective-permute-start | bytes 884744 | tf_op jit(solution)/shard_map/ppermute | solution.py:20
  90.3 3.4 %collective-permute-start.17 = (bf16[144,1024]{1,0:T(8,128)(2,1)S(1)}, bf16[144,1024]{1,0:T(8,128)(2,1)S(1)}, u32[]{:S(2)}, u32[]{:S(2)}) collective-permute-start(bf16[144,1024]{1,0:T(8,128)(2,1)S(1)} %slice_add_fusion.10), channel_id=1, source_target_pairs={{0,2},{2,4},{4,6},{6,8},{8,10},{10,12},{12,14},{14,16},{16,18},{18... | collective-permute-start | bytes 884744 | tf_op jit(solution)/shard_map/ppermute | solution.py:20
  95.7 5.1 %collective-permute-start.20 = (bf16[144,1024]{1,0:T(8,128)(2,1)S(1)}, bf16[144,1024]{1,0:T(8,128)(2,1)S(1)}, u32[]{:S(2)}, u32[]{:S(2)}) collective-permute-start(bf16[144,1024]{1,0:T(8,128)(2,1)S(1)} %collective-permute-done.16.refs_4_), channel_id=1, source_target_pairs={{0,30},{2,0},{4,2},{6,4},{8,6},{10,8},{12,10},{14,12},{16,14},{18,... | collective-permute-start | bytes 884744 | tf_op jit(solution)/shard_map/ppermute | solution.py:20
  100.9 2.4 %collective-permute-start.22 = (bf16[144,1024]{1,0:T(8,128)(2,1)S(1)}, bf16[144,1024]{1,0:T(8,128)(2,1)S(1)}, u32[]{:S(2)}, u32[]{:S(2)}) collective-permute-start(bf16[144,1024]{1,0:T(8,128)(2,1)S(1)} %slice_add_fusion.7), channel_id=1, source_target_pairs={{0,30},{2,0},{4,2},{6,4},{8,6},{10,8},{12,10},{14,12},{16,14},{18,... | collective-permute-start | bytes 884744 | tf_op jit(solution)/shard_map/ppermute | solution.py:20
  103.4 3.4 %collective-permute-start.21 = (bf16[144,1024]{1,0:T(8,128)(2,1)S(1)}, bf16[144,1024]{1,0:T(8,128)(2,1)S(1)}, u32[]{:S(2)}, u32[]{:S(2)}) collective-permute-start(bf16[144,1024]{1,0:T(8,128)(2,1)S(1)} %slice_add_fusion.8), channel_id=1, source_target_pairs={{0,2},{2,4},{4,6},{6,8},{8,10},{10,12},{12,14},{14,16},{16,18},{18... | collective-permute-start | bytes 884744 | tf_op jit(solution)/shard_map/ppermute | solution.py:20
  108.8 5.1 %collective-permute-start.24 = (bf16[144,1024]{1,0:T(8,128)(2,1)S(1)}, bf16[144,1024]{1,0:T(8,128)(2,1)S(1)}, u32[]{:S(2)}, u32[]{:S(2)}) collective-permute-start(bf16[144,1024]{1,0:T(8,128)(2,1)S(1)} %collective-permute-done.20.refs_5_), channel_id=1, source_target_pairs={{0,30},{2,0},{4,2},{6,4},{8,6},{10,8},{12,10},{14,12},{16,14},{18,... | collective-permute-start | bytes 884744 | tf_op jit(solution)/shard_map/ppermute | solution.py:20
  114.0 2.6 %collective-permute-start.26 = (bf16[144,1024]{1,0:T(8,128)(2,1)S(1)}, bf16[144,1024]{1,0:T(8,128)(2,1)S(1)}, u32[]{:S(2)}, u32[]{:S(2)}) collective-permute-start(bf16[144,1024]{1,0:T(8,128)(2,1)S(1)} %slice_add_fusion.5), channel_id=1, source_target_pairs={{0,30},{2,0},{4,2},{6,4},{8,6},{10,8},{12,10},{14,12},{16,14},{18,... | collective-permute-start | bytes 884744 | tf_op jit(solution)/shard_map/ppermute | solution.py:20
  116.6 3.2 %collective-permute-start.25 = (bf16[144,1024]{1,0:T(8,128)(2,1)S(1)}, bf16[144,1024]{1,0:T(8,128)(2,1)S(1)}, u32[]{:S(2)}, u32[]{:S(2)}) collective-permute-start(bf16[144,1024]{1,0:T(8,128)(2,1)S(1)} %slice_add_fusion.6), channel_id=1, source_target_pairs={{0,2},{2,4},{4,6},{6,8},{8,10},{10,12},{12,14},{14,16},{16,18},{18... | collective-permute-start | bytes 884744 | tf_op jit(solution)/shard_map/ppermute | solution.py:20
  121.8 5.1 %collective-permute-start.28 = (bf16[144,1024]{1,0:T(8,128)(2,1)S(1)}, bf16[144,1024]{1,0:T(8,128)(2,1)S(1)}, u32[]{:S(2)}, u32[]{:S(2)}) collective-permute-start(bf16[144,1024]{1,0:T(8,128)(2,1)S(1)} %collective-permute-done.24.refs_6_), channel_id=1, source_target_pairs={{0,30},{2,0},{4,2},{6,4},{8,6},{10,8},{12,10},{14,12},{16,14},{18,... | collective-permute-start | bytes 884744 | tf_op jit(solution)/shard_map/ppermute | solution.py:20
  127.1 2.6 %collective-permute-start.30 = (bf16[144,1024]{1,0:T(8,128)(2,1)S(1)}, bf16[144,1024]{1,0:T(8,128)(2,1)S(1)}, u32[]{:S(2)}, u32[]{:S(2)}) collective-permute-start(bf16[144,1024]{1,0:T(8,128)(2,1)S(1)} %slice_add_fusion.3), channel_id=1, source_target_pairs={{0,30},{2,0},{4,2},{6,4},{8,6},{10,8},{12,10},{14,12},{16,14},{18,... | collective-permute-start | bytes 884744 | tf_op jit(solution)/shard_map/ppermute | solution.py:20
  129.7 3.2 %collective-permute-start.29 = (bf16[144,1024]{1,0:T(8,128)(2,1)S(1)}, bf16[144,1024]{1,0:T(8,128)(2,1)S(1)}, u32[]{:S(2)}, u32[]{:S(2)}) collective-permute-start(bf16[144,1024]{1,0:T(8,128)(2,1)S(1)} %slice_add_fusion.4), channel_id=1, source_target_pairs={{0,2},{2,4},{4,6},{6,8},{8,10},{10,12},{12,14},{14,16},{16,18},{18... | collective-permute-start | bytes 884744 | tf_op jit(solution)/shard_map/ppermute | solution.py:20
  135.7 3.8 %collective-permute-done.29 = bf16[144,1024]{1,0:T(8,128)(2,1)S(1)} collective-permute-done((bf16[144,1024]{1,0:T(8,128)(2,1)S(1)}, bf16[144,1024]{1,0:T(8,128)(2,1)S(1)}, u32[]{:S(2)}, u32[]{:S(2)}) %collective-permute-start.29) | collective-permute-done | bytes 294944 | tf_op jit(solution)/shard_map/ppermute | solution.py:20
  139.5 2.3 %collective-permute-start.34 = (bf16[144,1024]{1,0:T(8,128)(2,1)S(1)}, bf16[144,1024]{1,0:T(8,128)(2,1)S(1)}, u32[]{:S(2)}, u32[]{:S(2)}) collective-permute-start(bf16[144,1024]{1,0:T(8,128)(2,1)S(1)} %slice_add_fusion.1), channel_id=1, source_target_pairs={{0,30},{2,0},{4,2},{6,4},{8,6},{10,8},{12,10},{14,12},{16,14},{18,... | collective-permute-start | bytes 884744 | tf_op jit(solution)/shard_map/ppermute | solution.py:20
  142.8 5.3 %shard_map.95 = (bf16[2304,128]{1,0:T(8,128)(2,1)S(1)}, bf16[3328,128]{1,0:T(8,128)(2,1)S(1)}, f32[128,1024]{1,0:T(8,128)S(1)}) custom-call(s32[2]{0:T(128)S(1)} %pad_add_fusion.at, bf16[2304,128]{1,0:T(8,128)(2,1)S(1)} %get-tuple-element.69.mine, bf16[3328,128]{1,0:T(8,128)(2,1)S(1)} %collective-permute-done.6.peer, ...), custom_call_target="tpu_custom_call" | custom-call | flops 2415919104 | bytes 4718592 | tf_op jit(solution)/shard_map/pallas_call | solution.py:36
  150.1 2.7 %collective-permute-start.33 = (bf16[144,1024]{1,0:T(8,128)(2,1)S(1)}, bf16[144,1024]{1,0:T(8,128)(2,1)S(1)}, u32[]{:S(2)}, u32[]{:S(2)}) collective-permute-start(bf16[144,1024]{1,0:T(8,128)(2,1)S(1)} %slice_add_fusion.2), channel_id=1, source_target_pairs={{0,2},{2,4},{4,6},{6,8},{8,10},{10,12},{12,14},{14,16},{16,18},{18... | collective-permute-start | bytes 884744 | tf_op jit(solution)/shard_map/ppermute | solution.py:20
  152.9 4.4 %collective-permute-start.35 = (bf16[144,1024]{1,0:T(8,128)(2,1)S(1)}, bf16[144,1024]{1,0:T(8,128)(2,1)S(1)}, u32[]{:S(2)}, u32[]{:S(2)}) collective-permute-start(bf16[144,1024]{1,0:T(8,128)(2,1)S(1)} %slice_add_fusion), channel_id=1, source_target_pairs={{0,30},{2,0},{4,2},{6,4},{8,6},{10,8},{12,10},{14,12},{16,14},{18,... | collective-permute-start | bytes 884744 | tf_op jit(solution)/shard_map/ppermute | solution.py:20
  163.5 2.1 %collective-permute-done.32.got = bf16[3328,128]{1,0:T(8,128)(2,1)S(1)} collective-permute-done((bf16[3328,128]{1,0:T(8,128)(2,1)S(1)}, bf16[3328,128]{1,0:T(8,128)(2,1)S(1)}, u32[]{:S(2)}, u32[]{:S(2)}) %collective-permute-start.32) | collective-permute-done | bytes 852000 | tf_op jit(solution)/shard_map/ppermute | solution.py:20
  165.5 2.9 %shard_map.96 = (bf16[128,1024]{1,0:T(8,128)(2,1)}, bf16[128,4608]{1,0:T(8,128)(2,1)}) custom-call(s32[2]{0:T(128)S(1)} %pad_add_fusion.at, bf16[2304,128]{1,0:T(8,128)(2,1)S(1)} %get-tuple-element.116.own, bf16[3328,128]{1,0:T(8,128)(2,1)S(1)} %collective-permute-done.32.got, bf16[128,4608]{1,0:T(8,128)(2,1)S(1)} %bitcast.17, f32[1,4608]{1,0:T(1,128)S(1)} %copy-done.7, ...), custom_call_target="tpu_custom_call" | custom-call | flops 5898240 | bytes 4718592 | tf_op jit(solution)/shard_map/pallas_call | solution.py:36
  (73 shorter events, 32.5 us)
Async XLA Ops:
  7.5 33.7 %collective-permute-start.6 = (bf16[3328,128]{1,0:T(8,128)(2,1)S(1)}, bf16[3328,128]{1,0:T(8,128)(2,1)S(1)}, u32[]{:S(2)}, u32[]{:S(2)}) collective-permute-start(bf16[3328,128]{1,0:T(8,128)(2,1)S(1)} %get-tuple-element.71), channel_id=1, source_target_pairs={{0,1},{1,0},{2,3},{3,2},{4,5},{5,4},{6,7},{7,6},{8,9},{9,8},{10,11... | collective-permute-start | bytes 2555912 | tf_op jit(solution)/shard_map/ppermute | solution.py:20
  11.6 29.7 %collective-permute-start.4 = (bf16[144,1024]{1,0:T(8,128)(2,1)S(1)}, bf16[144,1024]{1,0:T(8,128)(2,1)S(1)}, u32[]{:S(2)}, u32[]{:S(2)}) collective-permute-start(bf16[144,1024]{1,0:T(8,128)(2,1)S(1)} %get-tuple-element.70.refs_0_), channel_id=1, source_target_pairs={{0,2},{2,4},{4,6},{6,8},{8,10},{10,12},{12,14},{14,16},{16,18},{18... | collective-permute-start | bytes 884744 | tf_op jit(solution)/shard_map/ppermute | solution.py:20
  15.4 25.8 %collective-permute-start.5 = (bf16[144,1024]{1,0:T(8,128)(2,1)S(1)}, bf16[144,1024]{1,0:T(8,128)(2,1)S(1)}, u32[]{:S(2)}, u32[]{:S(2)}) collective-permute-start(bf16[144,1024]{1,0:T(8,128)(2,1)S(1)} %get-tuple-element.70.refs_0_), channel_id=1, source_target_pairs={{0,30},{2,0},{4,2},{6,4},{8,6},{10,8},{12,10},{14,12},{16,14},{18,... | collective-permute-start | bytes 884744 | tf_op jit(solution)/shard_map/ppermute | solution.py:20
  25.6 15.6 %collective-permute-start.1 = (bf16[160,1024]{1,0:T(8,128)(2,1)}, bf16[160,1024]{1,0:T(8,128)(2,1)}, u32[]{:S(2)}, u32[]{:S(2)}) collective-permute-start(bf16[160,1024]{1,0:T(8,128)(2,1)} %param.1), channel_id=1, source_target_pairs={{0,64},{32,96},{64,128},{96,160},{128,192},{160,224},{192,256},{22... | collective-permute-start | bytes 983048 | tf_op jit(solution)/shard_map/cond/branch_1_fun/ppermute | solution.py:20
  44.2 19.2 %collective-permute-start.7 = (bf16[144,1024]{1,0:T(8,128)(2,1)S(1)}, bf16[144,1024]{1,0:T(8,128)(2,1)S(1)}, u32[]{:S(2)}, u32[]{:S(2)}) collective-permute-start(bf16[144,1024]{1,0:T(8,128)(2,1)S(1)} %collective-permute-done.4.refs_15_), channel_id=1, source_target_pairs={{0,2},{2,4},{4,6},{6,8},{8,10},{10,12},{12,14},{14,16},{16,18},{18... | collective-permute-start | bytes 884744 | tf_op jit(solution)/shard_map/ppermute | solution.py:20
  48.0 17.3 %collective-permute-start.8 = (bf16[144,1024]{1,0:T(8,128)(2,1)S(1)}, bf16[144,1024]{1,0:T(8,128)(2,1)S(1)}, u32[]{:S(2)}, u32[]{:S(2)}) collective-permute-start(bf16[144,1024]{1,0:T(8,128)(2,1)S(1)} %collective-permute-done.5.refs_1_), channel_id=1, source_target_pairs={{0,30},{2,0},{4,2},{6,4},{8,6},{10,8},{12,10},{14,12},{16,14},{18,... | collective-permute-start | bytes 884744 | tf_op jit(solution)/shard_map/ppermute | solution.py:20
  57.5 13.0 %collective-permute-start.10 = (bf16[144,1024]{1,0:T(8,128)(2,1)S(1)}, bf16[144,1024]{1,0:T(8,128)(2,1)S(1)}, u32[]{:S(2)}, u32[]{:S(2)}) collective-permute-start(bf16[144,1024]{1,0:T(8,128)(2,1)S(1)} %slice.55), channel_id=1, source_target_pairs={{0,30},{2,0},{4,2},{6,4},{8,6},{10,8},{12,10},{14,12},{16,14},{18,... | collective-permute-start | bytes 884744 | tf_op jit(solution)/shard_map/ppermute | solution.py:20
  61.5 13.1 %collective-permute-start.9 = (bf16[144,1024]{1,0:T(8,128)(2,1)S(1)}, bf16[144,1024]{1,0:T(8,128)(2,1)S(1)}, u32[]{:S(2)}, u32[]{:S(2)}) collective-permute-start(bf16[144,1024]{1,0:T(8,128)(2,1)S(1)} %slice.54), channel_id=1, source_target_pairs={{0,2},{2,4},{4,6},{6,8},{8,10},{10,12},{12,14},{14,16},{16,18},{18... | collective-permute-start | bytes 884744 | tf_op jit(solution)/shard_map/ppermute | solution.py:20
  63.4 17.0 %collective-permute-start.11 = (bf16[144,1024]{1,0:T(8,128)(2,1)S(1)}, bf16[144,1024]{1,0:T(8,128)(2,1)S(1)}, u32[]{:S(2)}, u32[]{:S(2)}) collective-permute-start(bf16[144,1024]{1,0:T(8,128)(2,1)S(1)} %collective-permute-done.7.refs_14_), channel_id=1, source_target_pairs={{0,2},{2,4},{4,6},{6,8},{8,10},{10,12},{12,14},{14,16},{16,18},{18... | collective-permute-start | bytes 884744 | tf_op jit(solution)/shard_map/ppermute | solution.py:20
  65.3 15.1 %collective-permute-start.12 = (bf16[144,1024]{1,0:T(8,128)(2,1)S(1)}, bf16[144,1024]{1,0:T(8,128)(2,1)S(1)}, u32[]{:S(2)}, u32[]{:S(2)}) collective-permute-start(bf16[144,1024]{1,0:T(8,128)(2,1)S(1)} %collective-permute-done.8.refs_2_), channel_id=1, source_target_pairs={{0,30},{2,0},{4,2},{6,4},{8,6},{10,8},{12,10},{14,12},{16,14},{18,... | collective-permute-start | bytes 884744 | tf_op jit(solution)/shard_map/ppermute | solution.py:20
  74.5 13.0 %collective-permute-start.14 = (bf16[144,1024]{1,0:T(8,128)(2,1)S(1)}, bf16[144,1024]{1,0:T(8,128)(2,1)S(1)}, u32[]{:S(2)}, u32[]{:S(2)}) collective-permute-start(bf16[144,1024]{1,0:T(8,128)(2,1)S(1)} %slice_add_fusion.11), channel_id=1, source_target_pairs={{0,30},{2,0},{4,2},{6,4},{8,6},{10,8},{12,10},{14,12},{16,14},{18,... | collective-permute-start | bytes 884744 | tf_op jit(solution)/shard_map/ppermute | solution.py:20
  76.5 11.4 %collective-permute-start.13 = (bf16[144,1024]{1,0:T(8,128)(2,1)S(1)}, bf16[144,1024]{1,0:T(8,128)(2,1)S(1)}, u32[]{:S(2)}, u32[]{:S(2)}) collective-permute-start(bf16[144,1024]{1,0:T(8,128)(2,1)S(1)} %slice_add_fusion.12), channel_id=1, source_target_pairs={{0,2},{2,4},{4,6},{6,8},{8,10},{10,12},{12,14},{14,16},{16,18},{18... | collective-permute-start | bytes 884744 | tf_op jit(solution)/shard_map/ppermute | solution.py:20
  80.4 13.3 %collective-permute-start.15 = (bf16[144,1024]{1,0:T(8,128)(2,1)S(1)}, bf16[144,1024]{1,0:T(8,128)(2,1)S(1)}, u32[]{:S(2)}, u32[]{:S(2)}) collective-permute-start(bf16[144,1024]{1,0:T(8,128)(2,1)S(1)} %collective-permute-done.11.refs_13_), channel_id=1, source_target_pairs={{0,2},{2,4},{4,6},{6,8},{8,10},{10,12},{12,14},{14,16},{16,18},{18... | collective-permute-start | bytes 884744 | tf_op jit(solution)/shard_map/ppermute | solution.py:20
  82.4 11.4 %collective-permute-start.16 = (bf16[144,1024]{1,0:T(8,128)(2,1)S(1)}, bf16[144,1024]{1,0:T(8,128)(2,1)S(1)}, u32[]{:S(2)}, u32[]{:S(2)}) collective-permute-start(bf16[144,1024]{1,0:T(8,128)(2,1)S(1)} %collective-permute-done.12.refs_3_), channel_id=1, source_target_pairs={{0,30},{2,0},{4,2},{6,4},{8,6},{10,8},{12,10},{14,12},{16,14},{18,... | collective-permute-start | bytes 884744 | tf_op jit(solution)/shard_map/ppermute | solution.py:20
  87.9 13.0 %collective-permute-start.18 = (bf16[144,1024]{1,0:T(8,128)(2,1)S(1)}, bf16[144,1024]{1,0:T(8,128)(2,1)S(1)}, u32[]{:S(2)}, u32[]{:S(2)}) collective-permute-start(bf16[144,1024]{1,0:T(8,128)(2,1)S(1)} %slice_add_fusion.9), channel_id=1, source_target_pairs={{0,30},{2,0},{4,2},{6,4},{8,6},{10,8},{12,10},{14,12},{16,14},{18,... | collective-permute-start | bytes 884744 | tf_op jit(solution)/shard_map/ppermute | solution.py:20
  90.3 10.6 %collective-permute-start.17 = (bf16[144,1024]{1,0:T(8,128)(2,1)S(1)}, bf16[144,1024]{1,0:T(8,128)(2,1)S(1)}, u32[]{:S(2)}, u32[]{:S(2)}) collective-permute-start(bf16[144,1024]{1,0:T(8,128)(2,1)S(1)} %slice_add_fusion.10), channel_id=1, source_target_pairs={{0,2},{2,4},{4,6},{6,8},{8,10},{10,12},{12,14},{14,16},{16,18},{18... | collective-permute-start | bytes 884744 | tf_op jit(solution)/shard_map/ppermute | solution.py:20
  93.8 13.0 %collective-permute-start.19 = (bf16[144,1024]{1,0:T(8,128)(2,1)S(1)}, bf16[144,1024]{1,0:T(8,128)(2,1)S(1)}, u32[]{:S(2)}, u32[]{:S(2)}) collective-permute-start(bf16[144,1024]{1,0:T(8,128)(2,1)S(1)} %collective-permute-done.15.refs_12_), channel_id=1, source_target_pairs={{0,2},{2,4},{4,6},{6,8},{8,10},{10,12},{12,14},{14,16},{16,18},{18... | collective-permute-start | bytes 884744 | tf_op jit(solution)/shard_map/ppermute | solution.py:20
  95.7 11.1 %collective-permute-start.20 = (bf16[144,1024]{1,0:T(8,128)(2,1)S(1)}, bf16[144,1024]{1,0:T(8,128)(2,1)S(1)}, u32[]{:S(2)}, u32[]{:S(2)}) collective-permute-start(bf16[144,1024]{1,0:T(8,128)(2,1)S(1)} %collective-permute-done.16.refs_4_), channel_id=1, source_target_pairs={{0,30},{2,0},{4,2},{6,4},{8,6},{10,8},{12,10},{14,12},{16,14},{18,... | collective-permute-start | bytes 884744 | tf_op jit(solution)/shard_map/ppermute | solution.py:20
  100.9 13.0 %collective-permute-start.22 = (bf16[144,1024]{1,0:T(8,128)(2,1)S(1)}, bf16[144,1024]{1,0:T(8,128)(2,1)S(1)}, u32[]{:S(2)}, u32[]{:S(2)}) collective-permute-start(bf16[144,1024]{1,0:T(8,128)(2,1)S(1)} %slice_add_fusion.7), channel_id=1, source_target_pairs={{0,30},{2,0},{4,2},{6,4},{8,6},{10,8},{12,10},{14,12},{16,14},{18,... | collective-permute-start | bytes 884744 | tf_op jit(solution)/shard_map/ppermute | solution.py:20
  103.4 10.6 %collective-permute-start.21 = (bf16[144,1024]{1,0:T(8,128)(2,1)S(1)}, bf16[144,1024]{1,0:T(8,128)(2,1)S(1)}, u32[]{:S(2)}, u32[]{:S(2)}) collective-permute-start(bf16[144,1024]{1,0:T(8,128)(2,1)S(1)} %slice_add_fusion.8), channel_id=1, source_target_pairs={{0,2},{2,4},{4,6},{6,8},{8,10},{10,12},{12,14},{14,16},{16,18},{18... | collective-permute-start | bytes 884744 | tf_op jit(solution)/shard_map/ppermute | solution.py:20
  106.8 13.0 %collective-permute-start.23 = (bf16[144,1024]{1,0:T(8,128)(2,1)S(1)}, bf16[144,1024]{1,0:T(8,128)(2,1)S(1)}, u32[]{:S(2)}, u32[]{:S(2)}) collective-permute-start(bf16[144,1024]{1,0:T(8,128)(2,1)S(1)} %collective-permute-done.19.refs_11_), channel_id=1, source_target_pairs={{0,2},{2,4},{4,6},{6,8},{8,10},{10,12},{12,14},{14,16},{16,18},{18... | collective-permute-start | bytes 884744 | tf_op jit(solution)/shard_map/ppermute | solution.py:20
  108.8 11.1 %collective-permute-start.24 = (bf16[144,1024]{1,0:T(8,128)(2,1)S(1)}, bf16[144,1024]{1,0:T(8,128)(2,1)S(1)}, u32[]{:S(2)}, u32[]{:S(2)}) collective-permute-start(bf16[144,1024]{1,0:T(8,128)(2,1)S(1)} %collective-permute-done.20.refs_5_), channel_id=1, source_target_pairs={{0,30},{2,0},{4,2},{6,4},{8,6},{10,8},{12,10},{14,12},{16,14},{18,... | collective-permute-start | bytes 884744 | tf_op jit(solution)/shard_map/ppermute | solution.py:20
  114.0 13.0 %collective-permute-start.26 = (bf16[144,1024]{1,0:T(8,128)(2,1)S(1)}, bf16[144,1024]{1,0:T(8,128)(2,1)S(1)}, u32[]{:S(2)}, u32[]{:S(2)}) collective-permute-start(bf16[144,1024]{1,0:T(8,128)(2,1)S(1)} %slice_add_fusion.5), channel_id=1, source_target_pairs={{0,30},{2,0},{4,2},{6,4},{8,6},{10,8},{12,10},{14,12},{16,14},{18,... | collective-permute-start | bytes 884744 | tf_op jit(solution)/shard_map/ppermute | solution.py:20
  116.6 10.4 %collective-permute-start.25 = (bf16[144,1024]{1,0:T(8,128)(2,1)S(1)}, bf16[144,1024]{1,0:T(8,128)(2,1)S(1)}, u32[]{:S(2)}, u32[]{:S(2)}) collective-permute-start(bf16[144,1024]{1,0:T(8,128)(2,1)S(1)} %slice_add_fusion.6), channel_id=1, source_target_pairs={{0,2},{2,4},{4,6},{6,8},{8,10},{10,12},{12,14},{14,16},{16,18},{18... | collective-permute-start | bytes 884744 | tf_op jit(solution)/shard_map/ppermute | solution.py:20
  119.9 13.0 %collective-permute-start.27 = (bf16[144,1024]{1,0:T(8,128)(2,1)S(1)}, bf16[144,1024]{1,0:T(8,128)(2,1)S(1)}, u32[]{:S(2)}, u32[]{:S(2)}) collective-permute-start(bf16[144,1024]{1,0:T(8,128)(2,1)S(1)} %collective-permute-done.23.refs_10_), channel_id=1, source_target_pairs={{0,2},{2,4},{4,6},{6,8},{8,10},{10,12},{12,14},{14,16},{16,18},{18... | collective-permute-start | bytes 884744 | tf_op jit(solution)/shard_map/ppermute | solution.py:20
  121.8 11.1 %collective-permute-start.28 = (bf16[144,1024]{1,0:T(8,128)(2,1)S(1)}, bf16[144,1024]{1,0:T(8,128)(2,1)S(1)}, u32[]{:S(2)}, u32[]{:S(2)}) collective-permute-start(bf16[144,1024]{1,0:T(8,128)(2,1)S(1)} %collective-permute-done.24.refs_6_), channel_id=1, source_target_pairs={{0,30},{2,0},{4,2},{6,4},{8,6},{10,8},{12,10},{14,12},{16,14},{18,... | collective-permute-start | bytes 884744 | tf_op jit(solution)/shard_map/ppermute | solution.py:20
  127.1 8.6 %collective-permute-start.30 = (bf16[144,1024]{1,0:T(8,128)(2,1)S(1)}, bf16[144,1024]{1,0:T(8,128)(2,1)S(1)}, u32[]{:S(2)}, u32[]{:S(2)}) collective-permute-start(bf16[144,1024]{1,0:T(8,128)(2,1)S(1)} %slice_add_fusion.3), channel_id=1, source_target_pairs={{0,30},{2,0},{4,2},{6,4},{8,6},{10,8},{12,10},{14,12},{16,14},{18,... | collective-permute-start | bytes 884744 | tf_op jit(solution)/shard_map/ppermute | solution.py:20
  129.7 9.8 %collective-permute-start.29 = (bf16[144,1024]{1,0:T(8,128)(2,1)S(1)}, bf16[144,1024]{1,0:T(8,128)(2,1)S(1)}, u32[]{:S(2)}, u32[]{:S(2)}) collective-permute-start(bf16[144,1024]{1,0:T(8,128)(2,1)S(1)} %slice_add_fusion.4), channel_id=1, source_target_pairs={{0,2},{2,4},{4,6},{6,8},{8,10},{10,12},{12,14},{14,16},{16,18},{18... | collective-permute-start | bytes 884744 | tf_op jit(solution)/shard_map/ppermute | solution.py:20
  132.9 9.8 %collective-permute-start.31 = (bf16[144,1024]{1,0:T(8,128)(2,1)S(1)}, bf16[144,1024]{1,0:T(8,128)(2,1)S(1)}, u32[]{:S(2)}, u32[]{:S(2)}) collective-permute-start(bf16[144,1024]{1,0:T(8,128)(2,1)S(1)} %collective-permute-done.27.refs_9_), channel_id=1, source_target_pairs={{0,2},{2,4},{4,6},{6,8},{8,10},{10,12},{12,14},{14,16},{16,18},{18... | collective-permute-start | bytes 884744 | tf_op jit(solution)/shard_map/ppermute | solution.py:20
  139.5 13.3 %collective-permute-start.34 = (bf16[144,1024]{1,0:T(8,128)(2,1)S(1)}, bf16[144,1024]{1,0:T(8,128)(2,1)S(1)}, u32[]{:S(2)}, u32[]{:S(2)}) collective-permute-start(bf16[144,1024]{1,0:T(8,128)(2,1)S(1)} %slice_add_fusion.1), channel_id=1, source_target_pairs={{0,30},{2,0},{4,2},{6,4},{8,6},{10,8},{12,10},{14,12},{16,14},{18,... | collective-permute-start | bytes 884744 | tf_op jit(solution)/shard_map/ppermute | solution.py:20
  148.1 17.5 %collective-permute-start.32 = (bf16[3328,128]{1,0:T(8,128)(2,1)S(1)}, bf16[3328,128]{1,0:T(8,128)(2,1)S(1)}, u32[]{:S(2)}, u32[]{:S(2)}) collective-permute-start(bf16[3328,128]{1,0:T(8,128)(2,1)S(1)} %get-tuple-element.117), channel_id=1, source_target_pairs={{0,1},{1,0},{2,3},{3,2},{4,5},{5,4},{6,7},{7,6},{8,9},{9,8},{10,11... | collective-permute-start | bytes 2555912 | tf_op jit(solution)/shard_map/ppermute | solution.py:20
  150.1 9.8 %collective-permute-start.33 = (bf16[144,1024]{1,0:T(8,128)(2,1)S(1)}, bf16[144,1024]{1,0:T(8,128)(2,1)S(1)}, u32[]{:S(2)}, u32[]{:S(2)}) collective-permute-start(bf16[144,1024]{1,0:T(8,128)(2,1)S(1)} %slice_add_fusion.2), channel_id=1, source_target_pairs={{0,2},{2,4},{4,6},{6,8},{8,10},{10,12},{12,14},{14,16},{16,18},{18... | collective-permute-start | bytes 884744 | tf_op jit(solution)/shard_map/ppermute | solution.py:20
  (9 other events, 67.3 us)

commit v3 on v2

--- a/solution.py
+++ b/solution.py
@@ -84,19 +84,25 @@
         send[pl.ds(width // 2 + b * tokens, tokens), :] = grads[:, lanes(b)]
 
 
-def outer(rows, ring, at, mine, peer, grads, up, down, both):
+def product_at(rows, place, mine, peer, both):
+    of = block(rows, place)
+    normed = jnp.concatenate([mine[of, :], peer[of, :]], axis=1)
+    return jnp.dot(normed, both[...], preferred_element_type=f32).astype(bf16)
+
+
+def outer_far(rows, ring, at, mine, peer, grads, up, down, both):
     tokens, features = grads.shape
     both[pl.ds(0, tokens), :] = grads[...]
     for b in range(features // LANES):
         both[pl.ds(tokens, tokens), lanes(b)] = peer[pl.ds(mine.shape[0] + b * tokens, tokens), :]
-    for place in range(ring):
-        of = block(rows, place)
-        normed = jnp.concatenate([mine[of, :], peer[of, :]], axis=1)
-        product = jnp.dot(normed, both[...], preferred_element_type=f32).astype(bf16)
-        if place < ring // 2:
-            up[of, :] = product
-        else:
-            down[block(rows, place - ring // 2), :] = product
+    up[...] = product_at(rows, ring // 2 - 1, mine, peer, both)
+    down[...] = product_at(rows, ring // 2, mine, peer, both)
+
+
+def outer(rows, ring, at, mine, peer, both, up, down):
+    for i in range(ring // 2 - 1):
+        up[block(rows, i), :] = product_at(rows, i, mine, peer, both)
+        down[block(rows, i), :] = product_at(rows, ring // 2 + 1 + i, mine, peer, both)
 
 
 def project(rows, ring, at, mine, peer, both, *refs):
@@ -149,7 +155,7 @@
     rows, features = numer_rows.shape
     half, tail = width // 2, features // LANES * tokens
     work = 2 * tokens * width * features
-    arc = ((turns * rows, features), bf16)
+    arc = (((turns - 1) * rows, features), bf16)
 
     mine, send, inv_rms, param, message = call(
         partial(normalise, rows, ring),
@@ -180,15 +186,18 @@
         lax.rem(step_count[0], levels), [partial(sent, axis="gossip", distance=2**level) for level in range(levels)], message
     )
     peer, got = after_gather(1, peer, got)
-    part_up, part_down, both = call(
-        partial(outer, rows, ring), [arc, arc, ((2 * tokens, features), bf16)], (), work, 2 * half * features,
+    up, down, both = call(
+        partial(outer_far, rows, ring),
+        [((rows, features), bf16), ((rows, features), bf16), ((2 * tokens, features), bf16)],
+        (), work // turns, half * features // 4,
     )(at, mine, peer, grad_keys)
+    part_up, part_down = call(
+        partial(outer, rows, ring), [arc, arc], (), work, 2 * half * features,
+    )(at, mine, peer, both)
 
     def part(place):
-        array, i = (part_up, place) if place >= 0 else (part_down, place + turns)
+        array, i = (part_up, place) if place >= 0 else (part_down, place + turns - 1)
         return lax.slice_in_dim(array, i * rows, (i + 1) * rows)
-
-    up, down = part(turns - 1), part(-turns)
 
     def scatter(step, up, down):
         down = sent(down, "z", -1)

time: 170 us -> 166 us (0.976)
  the two profiles are of different devices: /device:TPU:2 before, /device:TPU:24 now
where the time goes in v3:
time: 166 us; the launch traced here: 165 us
  starting transfers between devices  115 us (69%)
  waiting for transfers between devices  24.6 us (15%)
  Pallas kernels  12.9 us (8%)
  local copies, waits for them, and re-layouts  5.21 us (3%)
  between operations  4.26 us (3%)
  other arithmetic  2.5 us (2%)
    ppermute x33, starting transfers between devices, sent(): lax.ppermute(block, axis, [(i, (i + distance) % count) for i in range(cou...  115 us
    ppermute x33, waiting for transfers between devices, sent(): lax.ppermute(block, axis, [(i, (i + distance) % count) for i in range(cou...  24.6 us
    pallas_call x5, Pallas kernels, run(): pl.pallas_call(body, out_shape=shapes, in_specs=[pl.BlockSpec(memory_spac...  12.9 us
    unnamed x16, local copies, waits for them, and re-layouts  4.03 us
  transfers between devices with their start and end apart: 33, of which 12 were waited for; matrix products, arithmetic and copies ran while one was open for 2% of the time, Pallas kernels for 5%

profile of v3, /device:TPU:24, one launch (start us, length us, event | category | flops | bytes accessed | tf_op | source)
XLA Modules:
  0.0 164.6 jit_solution(16918315167474173499)
XLA Ops:
  5.4 2.2 %shard_map.93 = (bf16[2304,128]{1,0:T(8,128)(2,1)S(1)}, bf16[3328,128]{1,0:T(8,128)(2,1)S(1)}, f32[128,1]{1,0:T(8,128)S(1)}, bf16[144,1024]{1,0:T(8,128)(2,1)S(1)}, bf16[160,1024]{1,0:T(8,128)(2,1)}) custom-call(s32[2]{0:T(128)S(1)} %pad_add_fusion.at, f32[1]{0:T(128)S(6)} %copy.14.push, bf16[128,4608]{1,0:T(8,128)(2,1)S(1)} %bitcast.16, ...), custom_call_target="tpu_custom_call" | custom-call | flops 5898240 | bytes 3538944 | tf_op jit(solution)/shard_map/pallas_call | solution.py:36
  7.5 4.9 %collective-permute-start.6 = (bf16[3328,128]{1,0:T(8,128)(2,1)S(1)}, bf16[3328,128]{1,0:T(8,128)(2,1)S(1)}, u32[]{:S(2)}, u32[]{:S(2)}) collective-permute-start(bf16[3328,128]{1,0:T(8,128)(2,1)S(1)} %get-tuple-element.73), channel_id=1, source_target_pairs={{0,1},{1,0},{2,3},{3,2},{4,5},{5,4},{6,7},{7,6},{8,9},{9,8},{10,11... | collective-permute-start | bytes 2555912 | tf_op jit(solution)/shard_map/ppermute | solution.py:20
  12.5 3.8 %collective-permute-start.4 = (bf16[144,1024]{1,0:T(8,128)(2,1)S(1)}, bf16[144,1024]{1,0:T(8,128)(2,1)S(1)}, u32[]{:S(2)}, u32[]{:S(2)}) collective-permute-start(bf16[144,1024]{1,0:T(8,128)(2,1)S(1)} %get-tuple-element.72.refs_0_), channel_id=1, source_target_pairs={{0,2},{2,4},{4,6},{6,8},{8,10},{10,12},{12,14},{14,16},{16,18},{18... | collective-permute-start | bytes 884744 | tf_op jit(solution)/shard_map/ppermute | solution.py:20
  16.3 9.5 %collective-permute-start.5 = (bf16[144,1024]{1,0:T(8,128)(2,1)S(1)}, bf16[144,1024]{1,0:T(8,128)(2,1)S(1)}, u32[]{:S(2)}, u32[]{:S(2)}) collective-permute-start(bf16[144,1024]{1,0:T(8,128)(2,1)S(1)} %get-tuple-element.72.refs_0_), channel_id=1, source_target_pairs={{0,30},{2,0},{4,2},{6,4},{8,6},{10,8},{12,10},{14,12},{16,14},{18,... | collective-permute-start | bytes 884744 | tf_op jit(solution)/shard_map/ppermute | solution.py:20
  26.5 8.7 %conditional.1 = (bf16[160,1024]{1,0:T(8,128)(2,1)}) conditional(s32[]{:T(128)} %clamp.3, bf16[160,1024]{1,0:T(8,128)(2,1)} %get-tuple-element.74, bf16[160,1024]{1,0:T(8,128)(2,1)} %get-tuple-element.74, bf16[160,1024]{1,0:T(8,128)(2,1)} %get-tuple-element.74, bf16[160,1024]{1,0:T(8,128)(2,1)} %get-tuple-element.74), branch_computations={%region_0.0_spmd, %region_1.0_spmd, %region_2.0_spmd, %region_3.0_... | conditional | bytes 1310768 | solution.py:185
  28.4 6.8 %collective-permute-done = bf16[160,1024]{1,0:T(8,128)(2,1)} collective-permute-done((bf16[160,1024]{1,0:T(8,128)(2,1)}, bf16[160,1024]{1,0:T(8,128)(2,1)}, u32[]{:S(2)}, u32[]{:S(2)}) %collective-permute-start) | collective-permute-done | bytes 327712 | tf_op jit(solution)/shard_map/cond/branch_0_fun/ppermute | solution.py:20
  37.1 8.9 %collective-permute-start.8 = (bf16[144,1024]{1,0:T(8,128)(2,1)S(1)}, bf16[144,1024]{1,0:T(8,128)(2,1)S(1)}, u32[]{:S(2)}, u32[]{:S(2)}) collective-permute-start(bf16[144,1024]{1,0:T(8,128)(2,1)S(1)} %collective-permute-done.5.refs_1_), channel_id=1, source_target_pairs={{0,30},{2,0},{4,2},{6,4},{8,6},{10,8},{12,10},{14,12},{16,14},{18,... | collective-permute-start | bytes 884744 | tf_op jit(solution)/shard_map/ppermute | solution.py:20
  47.0 3.9 %collective-permute-start.10 = (bf16[144,1024]{1,0:T(8,128)(2,1)S(1)}, bf16[144,1024]{1,0:T(8,128)(2,1)S(1)}, u32[]{:S(2)}, u32[]{:S(2)}) collective-permute-start(bf16[144,1024]{1,0:T(8,128)(2,1)S(1)} %get-tuple-element.84), channel_id=1, source_target_pairs={{0,30},{2,0},{4,2},{6,4},{8,6},{10,8},{12,10},{14,12},{16,14},{18,... | collective-permute-start | bytes 884744 | tf_op jit(solution)/shard_map/ppermute | solution.py:20
  56.6 5.1 %collective-permute-start.12 = (bf16[144,1024]{1,0:T(8,128)(2,1)S(1)}, bf16[144,1024]{1,0:T(8,128)(2,1)S(1)}, u32[]{:S(2)}, u32[]{:S(2)}) collective-permute-start(bf16[144,1024]{1,0:T(8,128)(2,1)S(1)} %collective-permute-done.8.refs_2_), channel_id=1, source_target_pairs={{0,30},{2,0},{4,2},{6,4},{8,6},{10,8},{12,10},{14,12},{16,14},{18,... | collective-permute-start | bytes 884744 | tf_op jit(solution)/shard_map/ppermute | solution.py:20
  61.8 2.1 %collective-permute-done.9 = bf16[144,1024]{1,0:T(8,128)(2,1)S(1)} collective-permute-done((bf16[144,1024]{1,0:T(8,128)(2,1)S(1)}, bf16[144,1024]{1,0:T(8,128)(2,1)S(1)}, u32[]{:S(2)}, u32[]{:S(2)}) %collective-permute-start.9) | collective-permute-done | bytes 294944 | tf_op jit(solution)/shard_map/ppermute | solution.py:20
  65.8 3.9 %collective-permute-start.13 = (bf16[144,1024]{1,0:T(8,128)(2,1)S(1)}, bf16[144,1024]{1,0:T(8,128)(2,1)S(1)}, u32[]{:S(2)}, u32[]{:S(2)}) collective-permute-start(bf16[144,1024]{1,0:T(8,128)(2,1)S(1)} %slice_add_fusion.12), channel_id=1, source_target_pairs={{0,2},{2,4},{4,6},{6,8},{8,10},{10,12},{12,14},{14,16},{16,18},{18... | collective-permute-start | bytes 884744 | tf_op jit(solution)/shard_map/ppermute | solution.py:20
  72.0 5.1 %collective-permute-start.16 = (bf16[144,1024]{1,0:T(8,128)(2,1)S(1)}, bf16[144,1024]{1,0:T(8,128)(2,1)S(1)}, u32[]{:S(2)}, u32[]{:S(2)}) collective-permute-start(bf16[144,1024]{1,0:T(8,128)(2,1)S(1)} %collective-permute-done.12.refs_3_), channel_id=1, source_target_pairs={{0,30},{2,0},{4,2},{6,4},{8,6},{10,8},{12,10},{14,12},{16,14},{18,... | collective-permute-start | bytes 884744 | tf_op jit(solution)/shard_map/ppermute | solution.py:20
  80.8 3.9 %collective-permute-start.17 = (bf16[144,1024]{1,0:T(8,128)(2,1)S(1)}, bf16[144,1024]{1,0:T(8,128)(2,1)S(1)}, u32[]{:S(2)}, u32[]{:S(2)}) collective-permute-start(bf16[144,1024]{1,0:T(8,128)(2,1)S(1)} %slice_add_fusion.10), channel_id=1, source_target_pairs={{0,2},{2,4},{4,6},{6,8},{8,10},{10,12},{12,14},{14,16},{16,18},{18... | collective-permute-start | bytes 884744 | tf_op jit(solution)/shard_map/ppermute | solution.py:20
  84.8 2.7 %collective-permute-start.19 = (bf16[144,1024]{1,0:T(8,128)(2,1)S(1)}, bf16[144,1024]{1,0:T(8,128)(2,1)S(1)}, u32[]{:S(2)}, u32[]{:S(2)}) collective-permute-start(bf16[144,1024]{1,0:T(8,128)(2,1)S(1)} %collective-permute-done.15.refs_12_), channel_id=1, source_target_pairs={{0,2},{2,4},{4,6},{6,8},{8,10},{10,12},{12,14},{14,16},{16,18},{18... | collective-permute-start | bytes 884744 | tf_op jit(solution)/shard_map/ppermute | solution.py:20
  87.5 4.5 %collective-permute-start.20 = (bf16[144,1024]{1,0:T(8,128)(2,1)S(1)}, bf16[144,1024]{1,0:T(8,128)(2,1)S(1)}, u32[]{:S(2)}, u32[]{:S(2)}) collective-permute-start(bf16[144,1024]{1,0:T(8,128)(2,1)S(1)} %collective-permute-done.16.refs_4_), channel_id=1, source_target_pairs={{0,30},{2,0},{4,2},{6,4},{8,6},{10,8},{12,10},{14,12},{16,14},{18,... | collective-permute-start | bytes 884744 | tf_op jit(solution)/shard_map/ppermute | solution.py:20
  93.9 2.2 %collective-permute-start.22 = (bf16[144,1024]{1,0:T(8,128)(2,1)S(1)}, bf16[144,1024]{1,0:T(8,128)(2,1)S(1)}, u32[]{:S(2)}, u32[]{:S(2)}) collective-permute-start(bf16[144,1024]{1,0:T(8,128)(2,1)S(1)} %slice_add_fusion.7), channel_id=1, source_target_pairs={{0,30},{2,0},{4,2},{6,4},{8,6},{10,8},{12,10},{14,12},{16,14},{18,... | collective-permute-start | bytes 884744 | tf_op jit(solution)/shard_map/ppermute | solution.py:20
  96.1 3.7 %collective-permute-start.21 = (bf16[144,1024]{1,0:T(8,128)(2,1)S(1)}, bf16[144,1024]{1,0:T(8,128)(2,1)S(1)}, u32[]{:S(2)}, u32[]{:S(2)}) collective-permute-start(bf16[144,1024]{1,0:T(8,128)(2,1)S(1)} %slice_add_fusion.8), channel_id=1, source_target_pairs={{0,2},{2,4},{4,6},{6,8},{8,10},{10,12},{12,14},{14,16},{16,18},{18... | collective-permute-start | bytes 884744 | tf_op jit(solution)/shard_map/ppermute | solution.py:20
  99.8 2.5 %collective-permute-start.23 = (bf16[144,1024]{1,0:T(8,128)(2,1)S(1)}, bf16[144,1024]{1,0:T(8,128)(2,1)S(1)}, u32[]{:S(2)}, u32[]{:S(2)}) collective-permute-start(bf16[144,1024]{1,0:T(8,128)(2,1)S(1)} %collective-permute-done.19.refs_11_), channel_id=1, source_target_pairs={{0,2},{2,4},{4,6},{6,8},{8,10},{10,12},{12,14},{14,16},{16,18},{18... | collective-permute-start | bytes 884744 | tf_op jit(solution)/shard_map/ppermute | solution.py:20
  102.3 4.6 %collective-permute-start.24 = (bf16[144,1024]{1,0:T(8,128)(2,1)S(1)}, bf16[144,1024]{1,0:T(8,128)(2,1)S(1)}, u32[]{:S(2)}, u32[]{:S(2)}) collective-permute-start(bf16[144,1024]{1,0:T(8,128)(2,1)S(1)} %collective-permute-done.20.refs_5_), channel_id=1, source_target_pairs={{0,30},{2,0},{4,2},{6,4},{8,6},{10,8},{12,10},{14,12},{16,14},{18,... | collective-permute-start | bytes 884744 | tf_op jit(solution)/shard_map/ppermute | solution.py:20
  106.9 2.1 %collective-permute-done.21 = bf16[144,1024]{1,0:T(8,128)(2,1)S(1)} collective-permute-done((bf16[144,1024]{1,0:T(8,128)(2,1)S(1)}, bf16[144,1024]{1,0:T(8,128)(2,1)S(1)}, u32[]{:S(2)}, u32[]{:S(2)}) %collective-permute-start.21) | collective-permute-done | bytes 294944 | tf_op jit(solution)/shard_map/ppermute | solution.py:20
  109.0 2.4 %collective-permute-start.26 = (bf16[144,1024]{1,0:T(8,128)(2,1)S(1)}, bf16[144,1024]{1,0:T(8,128)(2,1)S(1)}, u32[]{:S(2)}, u32[]{:S(2)}) collective-permute-start(bf16[144,1024]{1,0:T(8,128)(2,1)S(1)} %slice_add_fusion.5), channel_id=1, source_target_pairs={{0,30},{2,0},{4,2},{6,4},{8,6},{10,8},{12,10},{14,12},{16,14},{18,... | collective-permute-start | bytes 884744 | tf_op jit(solution)/shard_map/ppermute | solution.py:20
  111.4 3.5 %collective-permute-start.25 = (bf16[144,1024]{1,0:T(8,128)(2,1)S(1)}, bf16[144,1024]{1,0:T(8,128)(2,1)S(1)}, u32[]{:S(2)}, u32[]{:S(2)}) collective-permute-start(bf16[144,1024]{1,0:T(8,128)(2,1)S(1)} %slice_add_fusion.6), channel_id=1, source_target_pairs={{0,2},{2,4},{4,6},{6,8},{8,10},{10,12},{12,14},{14,16},{16,18},{18... | collective-permute-start | bytes 884744 | tf_op jit(solution)/shard_map/ppermute | solution.py:20
  116.8 5.1 %collective-permute-start.28 = (bf16[144,1024]{1,0:T(8,128)(2,1)S(1)}, bf16[144,1024]{1,0:T(8,128)(2,1)S(1)}, u32[]{:S(2)}, u32[]{:S(2)}) collective-permute-start(bf16[144,1024]{1,0:T(8,128)(2,1)S(1)} %collective-permute-done.24.refs_6_), channel_id=1, source_target_pairs={{0,30},{2,0},{4,2},{6,4},{8,6},{10,8},{12,10},{14,12},{16,14},{18,... | collective-permute-start | bytes 884744 | tf_op jit(solution)/shard_map/ppermute | solution.py:20
  122.0 2.8 %collective-permute-start.30 = (bf16[144,1024]{1,0:T(8,128)(2,1)S(1)}, bf16[144,1024]{1,0:T(8,128)(2,1)S(1)}, u32[]{:S(2)}, u32[]{:S(2)}) collective-permute-start(bf16[144,1024]{1,0:T(8,128)(2,1)S(1)} %slice_add_fusion.3), channel_id=1, source_target_pairs={{0,30},{2,0},{4,2},{6,4},{8,6},{10,8},{12,10},{14,12},{16,14},{18,... | collective-permute-start | bytes 884744 | tf_op jit(solution)/shard_map/ppermute | solution.py:20
  124.9 3.0 %collective-permute-start.29 = (bf16[144,1024]{1,0:T(8,128)(2,1)S(1)}, bf16[144,1024]{1,0:T(8,128)(2,1)S(1)}, u32[]{:S(2)}, u32[]{:S(2)}) collective-permute-start(bf16[144,1024]{1,0:T(8,128)(2,1)S(1)} %slice_add_fusion.4), channel_id=1, source_target_pairs={{0,2},{2,4},{4,6},{6,8},{8,10},{10,12},{12,14},{14,16},{16,18},{18... | collective-permute-start | bytes 884744 | tf_op jit(solution)/shard_map/ppermute | solution.py:20
  130.7 4.0 %collective-permute-done.29 = bf16[144,1024]{1,0:T(8,128)(2,1)S(1)} collective-permute-done((bf16[144,1024]{1,0:T(8,128)(2,1)S(1)}, bf16[144,1024]{1,0:T(8,128)(2,1)S(1)}, u32[]{:S(2)}, u32[]{:S(2)}) %collective-permute-start.29) | collective-permute-done | bytes 294944 | tf_op jit(solution)/shard_map/ppermute | solution.py:20
  134.7 2.4 %collective-permute-start.34 = (bf16[144,1024]{1,0:T(8,128)(2,1)S(1)}, bf16[144,1024]{1,0:T(8,128)(2,1)S(1)}, u32[]{:S(2)}, u32[]{:S(2)}) collective-permute-start(bf16[144,1024]{1,0:T(8,128)(2,1)S(1)} %slice_add_fusion.1), channel_id=1, source_target_pairs={{0,30},{2,0},{4,2},{6,4},{8,6},{10,8},{12,10},{14,12},{16,14},{18,... | collective-permute-start | bytes 884744 | tf_op jit(solution)/shard_map/ppermute | solution.py:20
  137.8 5.3 %shard_map.96 = (bf16[2304,128]{1,0:T(8,128)(2,1)S(1)}, bf16[3328,128]{1,0:T(8,128)(2,1)S(1)}, f32[128,1024]{1,0:T(8,128)S(1)}) custom-call(s32[2]{0:T(128)S(1)} %pad_add_fusion.at, bf16[2304,128]{1,0:T(8,128)(2,1)S(1)} %get-tuple-element.71.mine, bf16[3328,128]{1,0:T(8,128)(2,1)S(1)} %collective-permute-done.6.peer, ...), custom_call_target="tpu_custom_call" | custom-call | flops 2415919104 | bytes 4718592 | tf_op jit(solution)/shard_map/pallas_call | solution.py:36
  143.2 2.1 %collective-permute-start.32 = (bf16[3328,128]{1,0:T(8,128)(2,1)S(1)}, bf16[3328,128]{1,0:T(8,128)(2,1)S(1)}, u32[]{:S(2)}, u32[]{:S(2)}) collective-permute-start(bf16[3328,128]{1,0:T(8,128)(2,1)S(1)} %get-tuple-element.121), channel_id=1, source_target_pairs={{0,1},{1,0},{2,3},{3,2},{4,5},{5,4},{6,7},{7,6},{8,9},{9,8},{10,11... | collective-permute-start | bytes 2555912 | tf_op jit(solution)/shard_map/ppermute | solution.py:20
  145.2 2.9 %collective-permute-start.33 = (bf16[144,1024]{1,0:T(8,128)(2,1)S(1)}, bf16[144,1024]{1,0:T(8,128)(2,1)S(1)}, u32[]{:S(2)}, u32[]{:S(2)}) collective-permute-start(bf16[144,1024]{1,0:T(8,128)(2,1)S(1)} %slice_add_fusion.2), channel_id=1, source_target_pairs={{0,2},{2,4},{4,6},{6,8},{8,10},{10,12},{12,14},{14,16},{16,18},{18... | collective-permute-start | bytes 884744 | tf_op jit(solution)/shard_map/ppermute | solution.py:20
  148.2 4.2 %collective-permute-start.35 = (bf16[144,1024]{1,0:T(8,128)(2,1)S(1)}, bf16[144,1024]{1,0:T(8,128)(2,1)S(1)}, u32[]{:S(2)}, u32[]{:S(2)}) collective-permute-start(bf16[144,1024]{1,0:T(8,128)(2,1)S(1)} %slice_add_fusion), channel_id=1, source_target_pairs={{0,30},{2,0},{4,2},{6,4},{8,6},{10,8},{12,10},{14,12},{16,14},{18,... | collective-permute-start | bytes 884744 | tf_op jit(solution)/shard_map/ppermute | solution.py:20
  160.6 2.9 %shard_map.97 = (bf16[128,1024]{1,0:T(8,128)(2,1)}, bf16[128,4608]{1,0:T(8,128)(2,1)}) custom-call(s32[2]{0:T(128)S(1)} %pad_add_fusion.at, bf16[2304,128]{1,0:T(8,128)(2,1)S(1)} %get-tuple-element.120.own, bf16[3328,128]{1,0:T(8,128)(2,1)S(1)} %collective-permute-done.32.got, bf16[128,4608]{1,0:T(8,128)(2,1)S(1)} %bitcast.17, f32[1,4608]{1,0:T(1,128)S(1)} %copy-done.7, ...), custom_call_target="tpu_custom_call" | custom-call | flops 5898240 | bytes 4718592 | tf_op jit(solution)/shard_map/pallas_call | solution.py:36
  (72 shorter events, 37.3 us)
Async XLA Ops:
  7.5 27.7 %collective-permute-start.6 = (bf16[3328,128]{1,0:T(8,128)(2,1)S(1)}, bf16[3328,128]{1,0:T(8,128)(2,1)S(1)}, u32[]{:S(2)}, u32[]{:S(2)}) collective-permute-start(bf16[3328,128]{1,0:T(8,128)(2,1)S(1)} %get-tuple-element.73), channel_id=1, source_target_pairs={{0,1},{1,0},{2,3},{3,2},{4,5},{5,4},{6,7},{7,6},{8,9},{9,8},{10,11... | collective-permute-start | bytes 2555912 | tf_op jit(solution)/shard_map/ppermute | solution.py:20
  12.5 22.7 %collective-permute-start.4 = (bf16[144,1024]{1,0:T(8,128)(2,1)S(1)}, bf16[144,1024]{1,0:T(8,128)(2,1)S(1)}, u32[]{:S(2)}, u32[]{:S(2)}) collective-permute-start(bf16[144,1024]{1,0:T(8,128)(2,1)S(1)} %get-tuple-element.72.refs_0_), channel_id=1, source_target_pairs={{0,2},{2,4},{4,6},{6,8},{8,10},{10,12},{12,14},{14,16},{16,18},{18... | collective-permute-start | bytes 884744 | tf_op jit(solution)/shard_map/ppermute | solution.py:20
  16.3 18.9 %collective-permute-start.5 = (bf16[144,1024]{1,0:T(8,128)(2,1)S(1)}, bf16[144,1024]{1,0:T(8,128)(2,1)S(1)}, u32[]{:S(2)}, u32[]{:S(2)}) collective-permute-start(bf16[144,1024]{1,0:T(8,128)(2,1)S(1)} %get-tuple-element.72.refs_0_), channel_id=1, source_target_pairs={{0,30},{2,0},{4,2},{6,4},{8,6},{10,8},{12,10},{14,12},{16,14},{18,... | collective-permute-start | bytes 884744 | tf_op jit(solution)/shard_map/ppermute | solution.py:20
  26.5 8.7 %collective-permute-start = (bf16[160,1024]{1,0:T(8,128)(2,1)}, bf16[160,1024]{1,0:T(8,128)(2,1)}, u32[]{:S(2)}, u32[]{:S(2)}) collective-permute-start(bf16[160,1024]{1,0:T(8,128)(2,1)} %param), channel_id=1, source_target_pairs={{0,32},{32,64},{64,96},{96,128},{128,160},{160,192},{192,224},{224... | collective-permute-start | bytes 983048 | tf_op jit(solution)/shard_map/cond/branch_0_fun/ppermute | solution.py:20
  35.2 19.4 %collective-permute-start.7 = (bf16[144,1024]{1,0:T(8,128)(2,1)S(1)}, bf16[144,1024]{1,0:T(8,128)(2,1)S(1)}, u32[]{:S(2)}, u32[]{:S(2)}) collective-permute-start(bf16[144,1024]{1,0:T(8,128)(2,1)S(1)} %collective-permute-done.4.refs_15_), channel_id=1, source_target_pairs={{0,2},{2,4},{4,6},{6,8},{8,10},{10,12},{12,14},{14,16},{16,18},{18... | collective-permute-start | bytes 884744 | tf_op jit(solution)/shard_map/ppermute | solution.py:20
  37.1 19.4 %collective-permute-start.8 = (bf16[144,1024]{1,0:T(8,128)(2,1)S(1)}, bf16[144,1024]{1,0:T(8,128)(2,1)S(1)}, u32[]{:S(2)}, u32[]{:S(2)}) collective-permute-start(bf16[144,1024]{1,0:T(8,128)(2,1)S(1)} %collective-permute-done.5.refs_1_), channel_id=1, source_target_pairs={{0,30},{2,0},{4,2},{6,4},{8,6},{10,8},{12,10},{14,12},{16,14},{18,... | collective-permute-start | bytes 884744 | tf_op jit(solution)/shard_map/ppermute | solution.py:20
  47.0 14.7 %collective-permute-start.10 = (bf16[144,1024]{1,0:T(8,128)(2,1)S(1)}, bf16[144,1024]{1,0:T(8,128)(2,1)S(1)}, u32[]{:S(2)}, u32[]{:S(2)}) collective-permute-start(bf16[144,1024]{1,0:T(8,128)(2,1)S(1)} %get-tuple-element.84), channel_id=1, source_target_pairs={{0,30},{2,0},{4,2},{6,4},{8,6},{10,8},{12,10},{14,12},{16,14},{18,... | collective-permute-start | bytes 884744 | tf_op jit(solution)/shard_map/ppermute | solution.py:20
  50.9 13.0 %collective-permute-start.9 = (bf16[144,1024]{1,0:T(8,128)(2,1)S(1)}, bf16[144,1024]{1,0:T(8,128)(2,1)S(1)}, u32[]{:S(2)}, u32[]{:S(2)}) collective-permute-start(bf16[144,1024]{1,0:T(8,128)(2,1)S(1)} %get-tuple-element.82), channel_id=1, source_target_pairs={{0,2},{2,4},{4,6},{6,8},{8,10},{10,12},{12,14},{14,16},{16,18},{18... | collective-permute-start | bytes 884744 | tf_op jit(solution)/shard_map/ppermute | solution.py:20
  54.6 15.4 %collective-permute-start.11 = (bf16[144,1024]{1,0:T(8,128)(2,1)S(1)}, bf16[144,1024]{1,0:T(8,128)(2,1)S(1)}, u32[]{:S(2)}, u32[]{:S(2)}) collective-permute-start(bf16[144,1024]{1,0:T(8,128)(2,1)S(1)} %collective-permute-done.7.refs_14_), channel_id=1, source_target_pairs={{0,2},{2,4},{4,6},{6,8},{8,10},{10,12},{12,14},{14,16},{16,18},{18... | collective-permute-start | bytes 884744 | tf_op jit(solution)/shard_map/ppermute | solution.py:20
  56.6 13.5 %collective-permute-start.12 = (bf16[144,1024]{1,0:T(8,128)(2,1)S(1)}, bf16[144,1024]{1,0:T(8,128)(2,1)S(1)}, u32[]{:S(2)}, u32[]{:S(2)}) collective-permute-start(bf16[144,1024]{1,0:T(8,128)(2,1)S(1)} %collective-permute-done.8.refs_2_), channel_id=1, source_target_pairs={{0,30},{2,0},{4,2},{6,4},{8,6},{10,8},{12,10},{14,12},{16,14},{18,... | collective-permute-start | bytes 884744 | tf_op jit(solution)/shard_map/ppermute | solution.py:20
  63.9 13.2 %collective-permute-start.14 = (bf16[144,1024]{1,0:T(8,128)(2,1)S(1)}, bf16[144,1024]{1,0:T(8,128)(2,1)S(1)}, u32[]{:S(2)}, u32[]{:S(2)}) collective-permute-start(bf16[144,1024]{1,0:T(8,128)(2,1)S(1)} %slice_add_fusion.11), channel_id=1, source_target_pairs={{0,30},{2,0},{4,2},{6,4},{8,6},{10,8},{12,10},{14,12},{16,14},{18,... | collective-permute-start | bytes 884744 | tf_op jit(solution)/shard_map/ppermute | solution.py:20
  65.8 13.0 %collective-permute-start.13 = (bf16[144,1024]{1,0:T(8,128)(2,1)S(1)}, bf16[144,1024]{1,0:T(8,128)(2,1)S(1)}, u32[]{:S(2)}, u32[]{:S(2)}) collective-permute-start(bf16[144,1024]{1,0:T(8,128)(2,1)S(1)} %slice_add_fusion.12), channel_id=1, source_target_pairs={{0,2},{2,4},{4,6},{6,8},{8,10},{10,12},{12,14},{14,16},{16,18},{18... | collective-permute-start | bytes 884744 | tf_op jit(solution)/shard_map/ppermute | solution.py:20
  70.0 14.7 %collective-permute-start.15 = (bf16[144,1024]{1,0:T(8,128)(2,1)S(1)}, bf16[144,1024]{1,0:T(8,128)(2,1)S(1)}, u32[]{:S(2)}, u32[]{:S(2)}) collective-permute-start(bf16[144,1024]{1,0:T(8,128)(2,1)S(1)} %collective-permute-done.11.refs_13_), channel_id=1, source_target_pairs={{0,2},{2,4},{4,6},{6,8},{8,10},{10,12},{12,14},{14,16},{16,18},{18... | collective-permute-start | bytes 884744 | tf_op jit(solution)/shard_map/ppermute | solution.py:20
  72.0 12.8 %collective-permute-start.16 = (bf16[144,1024]{1,0:T(8,128)(2,1)S(1)}, bf16[144,1024]{1,0:T(8,128)(2,1)S(1)}, u32[]{:S(2)}, u32[]{:S(2)}) collective-permute-start(bf16[144,1024]{1,0:T(8,128)(2,1)S(1)} %collective-permute-done.12.refs_3_), channel_id=1, source_target_pairs={{0,30},{2,0},{4,2},{6,4},{8,6},{10,8},{12,10},{14,12},{16,14},{18,... | collective-permute-start | bytes 884744 | tf_op jit(solution)/shard_map/ppermute | solution.py:20
  78.9 13.2 %collective-permute-start.18 = (bf16[144,1024]{1,0:T(8,128)(2,1)S(1)}, bf16[144,1024]{1,0:T(8,128)(2,1)S(1)}, u32[]{:S(2)}, u32[]{:S(2)}) collective-permute-start(bf16[144,1024]{1,0:T(8,128)(2,1)S(1)} %slice_add_fusion.9), channel_id=1, source_target_pairs={{0,30},{2,0},{4,2},{6,4},{8,6},{10,8},{12,10},{14,12},{16,14},{18,... | collective-permute-start | bytes 884744 | tf_op jit(solution)/shard_map/ppermute | solution.py:20
  80.8 13.0 %collective-permute-start.17 = (bf16[144,1024]{1,0:T(8,128)(2,1)S(1)}, bf16[144,1024]{1,0:T(8,128)(2,1)S(1)}, u32[]{:S(2)}, u32[]{:S(2)}) collective-permute-start(bf16[144,1024]{1,0:T(8,128)(2,1)S(1)} %slice_add_fusion.10), channel_id=1, source_target_pairs={{0,2},{2,4},{4,6},{6,8},{8,10},{10,12},{12,14},{14,16},{16,18},{18... | collective-permute-start | bytes 884744 | tf_op jit(solution)/shard_map/ppermute | solution.py:20
  84.8 15.0 %collective-permute-start.19 = (bf16[144,1024]{1,0:T(8,128)(2,1)S(1)}, bf16[144,1024]{1,0:T(8,128)(2,1)S(1)}, u32[]{:S(2)}, u32[]{:S(2)}) collective-permute-start(bf16[144,1024]{1,0:T(8,128)(2,1)S(1)} %collective-permute-done.15.refs_12_), channel_id=1, source_target_pairs={{0,2},{2,4},{4,6},{6,8},{8,10},{10,12},{12,14},{14,16},{16,18},{18... | collective-permute-start | bytes 884744 | tf_op jit(solution)/shard_map/ppermute | solution.py:20
  87.5 12.2 %collective-permute-start.20 = (bf16[144,1024]{1,0:T(8,128)(2,1)S(1)}, bf16[144,1024]{1,0:T(8,128)(2,1)S(1)}, u32[]{:S(2)}, u32[]{:S(2)}) collective-permute-start(bf16[144,1024]{1,0:T(8,128)(2,1)S(1)} %collective-permute-done.16.refs_4_), channel_id=1, source_target_pairs={{0,30},{2,0},{4,2},{6,4},{8,6},{10,8},{12,10},{14,12},{16,14},{18,... | collective-permute-start | bytes 884744 | tf_op jit(solution)/shard_map/ppermute | solution.py:20
  93.9 13.0 %collective-permute-start.22 = (bf16[144,1024]{1,0:T(8,128)(2,1)S(1)}, bf16[144,1024]{1,0:T(8,128)(2,1)S(1)}, u32[]{:S(2)}, u32[]{:S(2)}) collective-permute-start(bf16[144,1024]{1,0:T(8,128)(2,1)S(1)} %slice_add_fusion.7), channel_id=1, source_target_pairs={{0,30},{2,0},{4,2},{6,4},{8,6},{10,8},{12,10},{14,12},{16,14},{18,... | collective-permute-start | bytes 884744 | tf_op jit(solution)/shard_map/ppermute | solution.py:20
  96.1 12.9 %collective-permute-start.21 = (bf16[144,1024]{1,0:T(8,128)(2,1)S(1)}, bf16[144,1024]{1,0:T(8,128)(2,1)S(1)}, u32[]{:S(2)}, u32[]{:S(2)}) collective-permute-start(bf16[144,1024]{1,0:T(8,128)(2,1)S(1)} %slice_add_fusion.8), channel_id=1, source_target_pairs={{0,2},{2,4},{4,6},{6,8},{8,10},{10,12},{12,14},{14,16},{16,18},{18... | collective-permute-start | bytes 884744 | tf_op jit(solution)/shard_map/ppermute | solution.py:20
  99.8 15.1 %collective-permute-start.23 = (bf16[144,1024]{1,0:T(8,128)(2,1)S(1)}, bf16[144,1024]{1,0:T(8,128)(2,1)S(1)}, u32[]{:S(2)}, u32[]{:S(2)}) collective-permute-start(bf16[144,1024]{1,0:T(8,128)(2,1)S(1)} %collective-permute-done.19.refs_11_), channel_id=1, source_target_pairs={{0,2},{2,4},{4,6},{6,8},{8,10},{10,12},{12,14},{14,16},{16,18},{18... | collective-permute-start | bytes 884744 | tf_op jit(solution)/shard_map/ppermute | solution.py:20
  102.3 12.6 %collective-permute-start.24 = (bf16[144,1024]{1,0:T(8,128)(2,1)S(1)}, bf16[144,1024]{1,0:T(8,128)(2,1)S(1)}, u32[]{:S(2)}, u32[]{:S(2)}) collective-permute-start(bf16[144,1024]{1,0:T(8,128)(2,1)S(1)} %collective-permute-done.20.refs_5_), channel_id=1, source_target_pairs={{0,30},{2,0},{4,2},{6,4},{8,6},{10,8},{12,10},{14,12},{16,14},{18,... | collective-permute-start | bytes 884744 | tf_op jit(solution)/shard_map/ppermute | solution.py:20
  109.0 13.0 %collective-permute-start.26 = (bf16[144,1024]{1,0:T(8,128)(2,1)S(1)}, bf16[144,1024]{1,0:T(8,128)(2,1)S(1)}, u32[]{:S(2)}, u32[]{:S(2)}) collective-permute-start(bf16[144,1024]{1,0:T(8,128)(2,1)S(1)} %slice_add_fusion.5), channel_id=1, source_target_pairs={{0,30},{2,0},{4,2},{6,4},{8,6},{10,8},{12,10},{14,12},{16,14},{18,... | collective-permute-start | bytes 884744 | tf_op jit(solution)/shard_map/ppermute | solution.py:20
  111.4 10.6 %collective-permute-start.25 = (bf16[144,1024]{1,0:T(8,128)(2,1)S(1)}, bf16[144,1024]{1,0:T(8,128)(2,1)S(1)}, u32[]{:S(2)}, u32[]{:S(2)}) collective-permute-start(bf16[144,1024]{1,0:T(8,128)(2,1)S(1)} %slice_add_fusion.6), channel_id=1, source_target_pairs={{0,2},{2,4},{4,6},{6,8},{8,10},{10,12},{12,14},{14,16},{16,18},{18... | collective-permute-start | bytes 884744 | tf_op jit(solution)/shard_map/ppermute | solution.py:20
  114.9 13.0 %collective-permute-start.27 = (bf16[144,1024]{1,0:T(8,128)(2,1)S(1)}, bf16[144,1024]{1,0:T(8,128)(2,1)S(1)}, u32[]{:S(2)}, u32[]{:S(2)}) collective-permute-start(bf16[144,1024]{1,0:T(8,128)(2,1)S(1)} %collective-permute-done.23.refs_10_), channel_id=1, source_target_pairs={{0,2},{2,4},{4,6},{6,8},{8,10},{10,12},{12,14},{14,16},{16,18},{18... | collective-permute-start | bytes 884744 | tf_op jit(solution)/shard_map/ppermute | solution.py:20
  116.8 11.1 %collective-permute-start.28 = (bf16[144,1024]{1,0:T(8,128)(2,1)S(1)}, bf16[144,1024]{1,0:T(8,128)(2,1)S(1)}, u32[]{:S(2)}, u32[]{:S(2)}) collective-permute-start(bf16[144,1024]{1,0:T(8,128)(2,1)S(1)} %collective-permute-done.24.refs_6_), channel_id=1, source_target_pairs={{0,30},{2,0},{4,2},{6,4},{8,6},{10,8},{12,10},{14,12},{16,14},{18,... | collective-permute-start | bytes 884744 | tf_op jit(solution)/shard_map/ppermute | solution.py:20
  122.0 8.6 %collective-permute-start.30 = (bf16[144,1024]{1,0:T(8,128)(2,1)S(1)}, bf16[144,1024]{1,0:T(8,128)(2,1)S(1)}, u32[]{:S(2)}, u32[]{:S(2)}) collective-permute-start(bf16[144,1024]{1,0:T(8,128)(2,1)S(1)} %slice_add_fusion.3), channel_id=1, source_target_pairs={{0,30},{2,0},{4,2},{6,4},{8,6},{10,8},{12,10},{14,12},{16,14},{18,... | collective-permute-start | bytes 884744 | tf_op jit(solution)/shard_map/ppermute | solution.py:20
  124.9 9.8 %collective-permute-start.29 = (bf16[144,1024]{1,0:T(8,128)(2,1)S(1)}, bf16[144,1024]{1,0:T(8,128)(2,1)S(1)}, u32[]{:S(2)}, u32[]{:S(2)}) collective-permute-start(bf16[144,1024]{1,0:T(8,128)(2,1)S(1)} %slice_add_fusion.4), channel_id=1, source_target_pairs={{0,2},{2,4},{4,6},{6,8},{8,10},{10,12},{12,14},{14,16},{16,18},{18... | collective-permute-start | bytes 884744 | tf_op jit(solution)/shard_map/ppermute | solution.py:20
  127.9 9.9 %collective-permute-start.31 = (bf16[144,1024]{1,0:T(8,128)(2,1)S(1)}, bf16[144,1024]{1,0:T(8,128)(2,1)S(1)}, u32[]{:S(2)}, u32[]{:S(2)}) collective-permute-start(bf16[144,1024]{1,0:T(8,128)(2,1)S(1)} %collective-permute-done.27.refs_9_), channel_id=1, source_target_pairs={{0,2},{2,4},{4,6},{6,8},{8,10},{10,12},{12,14},{14,16},{16,18},{18... | collective-permute-start | bytes 884744 | tf_op jit(solution)/shard_map/ppermute | solution.py:20
  134.7 13.4 %collective-permute-start.34 = (bf16[144,1024]{1,0:T(8,128)(2,1)S(1)}, bf16[144,1024]{1,0:T(8,128)(2,1)S(1)}, u32[]{:S(2)}, u32[]{:S(2)}) collective-permute-start(bf16[144,1024]{1,0:T(8,128)(2,1)S(1)} %slice_add_fusion.1), channel_id=1, source_target_pairs={{0,30},{2,0},{4,2},{6,4},{8,6},{10,8},{12,10},{14,12},{16,14},{18,... | collective-permute-start | bytes 884744 | tf_op jit(solution)/shard_map/ppermute | solution.py:20
  143.2 17.4 %collective-permute-start.32 = (bf16[3328,128]{1,0:T(8,128)(2,1)S(1)}, bf16[3328,128]{1,0:T(8,128)(2,1)S(1)}, u32[]{:S(2)}, u32[]{:S(2)}) collective-permute-start(bf16[3328,128]{1,0:T(8,128)(2,1)S(1)} %get-tuple-element.121), channel_id=1, source_target_pairs={{0,1},{1,0},{2,3},{3,2},{4,5},{5,4},{6,7},{7,6},{8,9},{9,8},{10,11... | collective-permute-start | bytes 2555912 | tf_op jit(solution)/shard_map/ppermute | solution.py:20
  145.2 9.8 %collective-permute-start.33 = (bf16[144,1024]{1,0:T(8,128)(2,1)S(1)}, bf16[144,1024]{1,0:T(8,128)(2,1)S(1)}, u32[]{:S(2)}, u32[]{:S(2)}) collective-permute-start(bf16[144,1024]{1,0:T(8,128)(2,1)S(1)} %slice_add_fusion.2), channel_id=1, source_target_pairs={{0,2},{2,4},{4,6},{6,8},{8,10},{10,12},{12,14},{14,16},{16,18},{18... | collective-permute-start | bytes 884744 | tf_op jit(solution)/shard_map/ppermute | solution.py:20
  (9 other events, 110.3 us)
